TPU v7x, 32 devices: a whole 2x2x4 slice. The times are simulated.
32 devices in a mesh: owner: 16 (over z, y, x), pair: 2 (over core).
Axes of the slice: x: 2, y: 2, z: 4, core: 2. Of those that a mesh axis runs over, the one named last changes fastest.
Arguments:
- incident: float32 [32, 2, 32, 512], P('owner', None, None, 'pair'), may hold values from -6 to 6
- tmat: float32 [32, 2, 512, 512], P('owner', None, 'pair'), may hold values from -0.1875 to 0.1875
- blocks: float32 [336, 2, 512, 512], P('owner', None, None, 'pair'), may hold values from -0.09375 to 0.09375
- block_rows: int32 [336], P('owner'), may hold values from 0 to 1
- partners: int32 [336], replicated, may hold values from 0 to 31, as said below
- live: int32 [16], P('owner'), may hold values from 1 to 21, as said below
- owner_of: int32 [32], replicated, may hold values from 0 to 31, as said below
Outputs:
- scattered: float32 [32, 2, 32, 512], P('owner', None, None, 'pair')
- exciting: float32 [32, 2, 32, 512], P('owner', None, None, 'pair')
Inputs may be any that keep to these rules, and one draw needn't show every extreme that they name: A permutation: particle p's coefficients and T-matrix stand in row owner_of[p]. `partners`: the 21 slots of one owner name distinct particles whose rows lie with owners either less than 7 positions away on either side around the cycle of owners or exactly 8 positions away, never the owner itself, at most 2 with any one other owner; for every owner some other owner holds exactly 2 of them. Slots n with n mod 21 below live[n // 21] are live; some owner has all 21 slots live.
All inputs are finite; a program needn't handle non-finite values.
Results may differ from a plain program's by a relative error of at most 0.0003.
Values sent between devices are 32-bit elements; how exact they have to be, the bound alone decides.
No kernel may reach another device: no remote copies, remote signals or barrier semaphores. Data moves between devices by JAX's collectives and lax.ppermute only.
A program may use at most 128 MiB of HBM per device.

v0:
```python
import functools

import jax
import jax.numpy as jnp
from jax import lax
from jax.experimental import pallas as pl
from jax.experimental.pallas import tpu as pltpu
from jax.sharding import PartitionSpec as P

ITERS = 2
COLUMNS = 4
BUFFERS = 4
F32 = jnp.float32
BF16 = jnp.bfloat16
MIB = 1 << 20
STREAM_LIMIT = 48 * MIB
ALONE_LIMIT = 63 * MIB
GROUPS = 5
VMEM = pl.BlockSpec(memory_space=pltpu.VMEM)
SMEM = pl.BlockSpec(memory_space=pltpu.SMEM)
ANY = pl.BlockSpec(memory_space=pl.ANY)
HBM = pl.BlockSpec(memory_space=pltpu.MemorySpace.HBM)


def split_value(value):
    high = value.astype(BF16)
    low = (value - high.astype(F32)).astype(BF16)
    return high, low


def stacked_parts(real, imag):
    real_high, real_low = split_value(real)
    imag_high, imag_low = split_value(imag)
    with_real = jnp.concatenate((real_high, imag_high, real_low, imag_low), axis=0)
    with_imag = jnp.concatenate((-imag_high, real_high, -imag_low, real_low), axis=0)
    return with_real, with_imag


def dot_nt(left, right):
    return lax.dot_general(left, right, (((1,), (1,)), ((), ())), preferred_element_type=F32)


def dot_nn(left, right):
    return jnp.dot(left, right, preferred_element_type=F32)


def params(*byte_counts):
    return pltpu.CompilerParams(vmem_limit_bytes=sum(byte_counts) + 6 * MIB)


def size_of(*arrays):
    return sum(value.size * value.dtype.itemsize for value in arrays)


def place_of(column, particle, layer, particles, layers):
    return (column * particles + particle) * layers + layer


def index_kernel(
    layers, particles, owner_ref, side_ref, partners_ref, rows_of_ref, holders_ref, live_ref, *refs
):
    index_ref = refs[-1]
    slots = holders_ref.shape[0]
    stride, counts = GROUPS * slots, 3 * GROUPS * slots
    me = owner_ref[0]
    my_column, my_layer = lax.rem(me, COLUMNS), lax.div(me, COLUMNS)
    for group in range(GROUPS):
        index_ref[counts + group] = 0
    index_ref[counts + GROUPS] = side_ref[0]

    def step(slot, carry):
        row = rows_of_ref[partners_ref[me * slots + slot]]
        owner, particle = lax.div(row, particles), lax.rem(row, particles)
        column = lax.bitwise_xor(lax.rem(owner, COLUMNS), my_column)
        layer = lax.bitwise_xor(lax.div(owner, COLUMNS), my_layer)
        near = jnp.where(column == COLUMNS - 1, 2, 1)
        far = jnp.where(column == COLUMNS - 1, 4, 3)
        group = jnp.where(column == 0, 0, jnp.where(layer == 0, near, far))
        found = index_ref[counts + group]
        index_ref[counts + group] = found + 1
        position = group * slots + found
        index_ref[position] = slot
        index_ref[stride + position] = place_of(column, particle, layer, particles, layers)
        index_ref[2 * stride + position] = holders_ref[slot]
        return carry

    lax.fori_loop(0, live_ref[0], step, 0)


def slot_index(my_owner, side, partners, owner_of, block_rows, live, layers, particles):
    slots = block_rows.shape[0]
    return pl.pallas_call(
        functools.partial(index_kernel, layers, particles),
        out_shape=jax.ShapeDtypeStruct((3 * GROUPS * slots + GROUPS + 1,), jnp.int32),
        in_specs=[SMEM] * 6,
        out_specs=SMEM,
        compiler_params=pltpu.CompilerParams(vmem_limit_bytes=ALONE_LIMIT),
        name="slot_index",
    )(my_owner, side, partners, owner_of, block_rows, live)


def prepare_kernel(tmat_ref, incident_ref, after_ref, parts_ref, copy_ref, buf_ref, sems):
    particles, _, half, width = tmat_ref.shape

    def fetch(row):
        return pltpu.make_async_copy(tmat_ref.at[row], buf_ref.at[row], sems.at[row])

    for row in range(particles):
        fetch(row).start()
    own = pltpu.make_async_copy(incident_ref, copy_ref, sems.at[particles])
    own.start()
    for row in range(particles):
        fetch(row).wait()
        for part in range(2):
            high, low = split_value(buf_ref[row, part])
            parts_ref[row, :, part * width : (part + 1) * width] = high
            parts_ref[row, :, (2 + part) * width : (3 + part) * width] = low
    own.wait()


def prepare(tmat, incident, after):
    particles, _, half, width = tmat.shape
    return pl.pallas_call(
        prepare_kernel,
        out_shape=(
            jax.ShapeDtypeStruct((particles, half, 4 * width), BF16),
            jax.ShapeDtypeStruct(incident.shape, F32),
        ),
        in_specs=[HBM, HBM, ANY],
        out_specs=(VMEM, VMEM),
        scratch_shapes=[pltpu.VMEM(tmat.shape, F32), pltpu.SemaphoreType.DMA((particles + 1,))],
        compiler_params=params(2 * size_of(tmat), size_of(incident)),
        name="prepare",
    )(tmat, incident, after)


def tmat_kernel(halves, side_ref, mine_ref, theirs_ref, parts_ref, *refs):
    last = len(refs) == 4
    exciting_ref = refs[0] if last else None
    scattered_ref, full_ref = refs[1:3] if last else refs
    particles, _, directions, width = full_ref.shape
    half = width // 2
    start = pl.multiple_of(side_ref[0] * half, half)
    if halves:
        full_ref[:, :, :, pl.ds(start, half)] = mine_ref[...]
        full_ref[:, :, :, pl.ds(pl.multiple_of(half - start, half), half)] = theirs_ref[...]
    else:
        full_ref[...] = mine_ref[...] + theirs_ref[...]
    if last:
        window = full_ref.at[:, :, :, pl.ds(start, half)]
        leave = pltpu.make_async_copy(window, exciting_ref, refs[3])
        leave.start()
    for row in range(particles):
        with_real, with_imag = stacked_parts(full_ref[row, 0], full_ref[row, 1])
        right = jnp.concatenate((with_real, with_imag, with_real, with_imag), axis=1)
        total = dot_nt(parts_ref[row], right)
        out = (total[:, : 2 * directions] + total[:, 2 * directions :]).T
        scattered_ref[row, 0] = out[:directions]
        scattered_ref[row, 1] = out[directions:]
    if last:
        leave.wait()


def apply_tmat(halves, last, side, mine, theirs, parts):
    particles, _, directions, _ = mine.shape
    half = parts.shape[1]
    half_shape = jax.ShapeDtypeStruct((particles, 2, directions, half), F32)
    scratch = [pltpu.VMEM((particles, 2, directions, 2 * half), F32)]
    if last:
        scratch.append(pltpu.SemaphoreType.DMA)
    return pl.pallas_call(
        functools.partial(tmat_kernel, halves),
        out_shape=[half_shape] * (2 if last else 1),
        in_specs=[SMEM, VMEM, VMEM, VMEM],
        out_specs=[HBM, VMEM] if last else [VMEM],
        scratch_shapes=scratch,
        compiler_params=params(3 * size_of(mine, theirs), size_of(parts)),
        name="tmat_apply",
    )(side, mine, theirs, parts)


def chosen_slots(index_ref, groups, slots):
    stride, counts = GROUPS * slots, 3 * GROUPS * slots
    starts, total = [], 0
    for group in groups:
        starts.append(total)
        total = total + index_ref[counts + group]

    def at_turn(turn):
        position = groups[0] * slots + turn
        for group, start in zip(groups[1:], starts[1:]):
            position = jnp.where(turn >= start, group * slots + turn - start, position)
        return [index_ref[number * stride + position] for number in range(3)]

    return total, at_turn


def backward_kernel(first, groups, base, index_ref, own_ref, other_ref, blocks_ref, *refs):
    if first:
        out_ref, parts_ref, left_ref, buf_ref, sems, made_ref, made_sems = refs[-7:]
    else:
        out_ref, left_ref, buf_ref, sems = refs
    directions, half = own_ref.shape[2], own_ref.shape[3]
    width = 2 * half
    slots = blocks_ref.shape[0]
    wanted, at_turn = chosen_slots(index_ref, groups, slots)
    own_side = index_ref[3 * GROUPS * slots + GROUPS]

    def fetch(turn, place):
        return pltpu.make_async_copy(
            blocks_ref.at[at_turn(turn)[0]], buf_ref.at[place], sems.at[place]
        )

    def keep(turn, place):
        return pltpu.make_async_copy(
            made_ref.at[place], parts_ref.at[at_turn(turn)[0]], made_sems.at[place]
        )

    for early in range(BUFFERS):

        @pl.when(early < wanted)
        def _():
            fetch(early, early).start()

    for field_ref, side in ((own_ref, own_side), (other_ref, 1 - own_side)):
        for row in range(other_ref.shape[0]):
            with_real, with_imag = stacked_parts(field_ref[row, 0], field_ref[row, 1])
            for part, value in enumerate((with_real, with_imag)):
                start = pl.multiple_of(part * width + side * half, half)
                left_ref[row, :, pl.ds(start, half)] = value
    out_ref[...] = jnp.zeros_like(out_ref)

    def body(turn, carry):
        here = lax.rem(turn, BUFFERS)
        fetch(turn, here).wait()
        _, place, holder = at_turn(turn)
        place = place - base
        if first:
            spot = lax.rem(turn, 2)

            @pl.when(turn >= 2)
            def _():
                keep(turn - 2, spot).wait()

            high, low = split_value(buf_ref[here].reshape(2 * width, half))
            made_ref[spot, 0] = high.reshape(2, width, half)
            made_ref[spot, 1] = low.reshape(2, width, half)
            keep(turn, spot).start()
        else:
            high = buf_ref[here, 0].reshape(2 * width, half)
            low = buf_ref[here, 1].reshape(2 * width, half)
        total = dot_nn(left_ref[holder], high)
        rest = dot_nn(left_ref[holder, : 2 * directions], low)
        out = total[: 2 * directions] + total[2 * directions :] + rest
        out_ref[place, 0] = out[:directions]
        out_ref[place, 1] = out[directions:]

        @pl.when(turn + BUFFERS < wanted)
        def _():
            fetch(turn + BUFFERS, here).start()

        return carry

    lax.fori_loop(0, wanted, body, 0)
    if first:

        @pl.when(wanted >= 2)
        def _():
            keep(wanted - 2, lax.rem(wanted, 2)).wait()

        @pl.when(wanted >= 1)
        def _():
            keep(wanted - 1, lax.rem(wanted - 1, 2)).wait()


def backward(first, groups, base, count, index, own_half, other_half, blocks, parts):
    particles, _, directions, half = other_half.shape
    width = 2 * half
    slots = blocks.shape[0]
    out_shape = [jax.ShapeDtypeStruct((count, 2, directions, half), F32)]
    out_specs = [VMEM]
    source = blocks if first else parts
    scratch = [
        pltpu.VMEM((particles, 4 * directions, 2 * width), BF16),
        pltpu.VMEM((BUFFERS,) + source.shape[1:], source.dtype),
        pltpu.SemaphoreType.DMA((BUFFERS,)),
    ]
    operands = [index, own_half, other_half, source]
    in_specs = [SMEM, VMEM, VMEM, HBM]
    aliases = {}
    if first:
        out_shape.append(jax.ShapeDtypeStruct((slots, 2, 2, width, half), BF16))
        out_specs.append(HBM)
        scratch.append(pltpu.VMEM((2, 2, 2, width, half), BF16))
        scratch.append(pltpu.SemaphoreType.DMA((2,)))
        if parts is not None:
            aliases = {len(operands): 1}
            operands.append(parts)
            in_specs.append(HBM)
    return pl.pallas_call(
        functools.partial(backward_kernel, first, groups, base),
        out_shape=out_shape,
        in_specs=in_specs,
        out_specs=out_specs,
        scratch_shapes=scratch,
        input_output_aliases=aliases,
        compiler_params=pltpu.CompilerParams(vmem_limit_bytes=STREAM_LIMIT),
        cost_estimate=pl.CostEstimate(
            flops=directions * width * half,
            bytes_accessed=size_of(own_half),
            transcendentals=0,
        ),
        name="backward_group" + str(groups[0]),
    )(*operands)


def forward_kernel(groups, copies, count, begun, last, index_ref, *refs):
    field_refs = refs[:count]
    parts_ref = refs[count]
    if last:
        out_ref, every_ref, buf_ref, sems, acc_ref = refs[-5:]
    else:
        acc_ref, every_ref, buf_ref, sems = refs[-4:]
    directions = every_ref.shape[2]
    wanted, at_turn = chosen_slots(index_ref, groups, parts_ref.shape[0])

    def fetch(turn, place):
        return pltpu.make_async_copy(
            parts_ref.at[at_turn(turn)[0]], buf_ref.at[place], sems.at[place]
        )

    for early in range(BUFFERS):

        @pl.when(early < wanted)
        def _():
            fetch(early, early).start()

    acc_ref[...] = refs[count + 1][...] if begun else jnp.zeros_like(acc_ref)
    for number, row, place in copies:
        every_ref[place] = field_refs[number][row]

    def body(turn, carry):
        here = lax.rem(turn, BUFFERS)
        _, place, holder = at_turn(turn)
        with_real, with_imag = stacked_parts(every_ref[place, 0], every_ref[place, 1])
        fetch(turn, here).wait()
        total = dot_nt(buf_ref[here, 0, 0], with_real) + dot_nt(buf_ref[here, 0, 1], with_imag)
        total += dot_nt(buf_ref[here, 1, 0], with_real) + dot_nt(buf_ref[here, 1, 1], with_imag)
        acc_ref[holder] += total

        @pl.when(turn + BUFFERS < wanted)
        def _():
            fetch(turn + BUFFERS, here).start()

        return carry

    lax.fori_loop(0, wanted, body, 0)
    for row in range(acc_ref.shape[0] if last else 0):
        total = acc_ref[row]
        out = (total[:, : 2 * directions] + total[:, 2 * directions :]).T
        out_ref[row, 0] = out[:directions]
        out_ref[row, 1] = out[directions:]


def forward(groups, index, fields, copies, parts, particles, total_rows, before, last, after):
    slots, _, _, width, half = parts.shape
    directions = fields[0].shape[2]
    acc = (particles, width, 4 * directions)
    given = [] if before is None else [before]
    scratch = [
        pltpu.VMEM((total_rows, 2, directions, half), F32),
        pltpu.VMEM((BUFFERS,) + parts.shape[1:], BF16),
        pltpu.SemaphoreType.DMA((BUFFERS,)),
    ]
    if last:
        scratch.append(pltpu.VMEM(acc, F32))
    out_shape = jax.ShapeDtypeStruct((particles, 2, directions, width) if last else acc, F32)
    return pl.pallas_call(
        functools.partial(forward_kernel, groups, copies, len(fields), bool(given), last),
        out_shape=out_shape,
        in_specs=[SMEM] + [VMEM] * len(fields) + [HBM] + [VMEM] * len(given) + [ANY] * len(after),
        out_specs=VMEM,
        scratch_shapes=scratch,
        compiler_params=pltpu.CompilerParams(vmem_limit_bytes=STREAM_LIMIT),
        cost_estimate=pl.CostEstimate(
            flops=directions * width * half,
            bytes_accessed=size_of(out_shape),
            transcendentals=0,
        ),
        name="forward_group" + str(groups[0]),
    )(index, *fields, parts, *given, *after)


def pack_kernel(plans, count, *refs):
    in_refs, out_refs = refs[:count], refs[-len(plans) :]
    for out_ref, plan in zip(out_refs, plans):
        for row, terms in enumerate(plan):
            value = in_refs[terms[0][0]][terms[0][1]]
            for number, source in terms[1:]:
                value = value + in_refs[number][source]
            out_ref[row] = value


def pack(name, inputs, plans, after=()):
    shapes = [jax.ShapeDtypeStruct((len(plan),) + inputs[0].shape[1:], F32) for plan in plans]
    return pl.pallas_call(
        functools.partial(pack_kernel, plans, len(inputs)),
        out_shape=shapes,
        in_specs=[VMEM] * len(inputs) + [ANY] * len(after),
        out_specs=[VMEM] * len(plans),
        compiler_params=params(size_of(*inputs), size_of(*shapes)),
        name=name,
    )(*inputs, *after)


def total_kernel(counts, side_ref, incident_ref, *refs):
    nears, halves, out_ref = refs[: counts[0]], refs[counts[0] : -1], refs[-1]
    particles, half = incident_ref.shape[0], incident_ref.shape[3]
    start = pl.multiple_of(side_ref[0] * half, half)
    near = nears[0][...]
    for ref in nears[1:]:
        near = near + ref[...]
    out_ref[...] = near
    for particle in range(particles):
        value = incident_ref[particle]
        for ref, step in zip(halves, counts[1]):
            value = value + ref[particle * step]
        window = (particle, slice(None), slice(None), pl.ds(start, half))
        out_ref[window] = out_ref[window] + value


def whole_total(side, incident, nears, halves):
    arrays = [value for value, _ in halves]
    steps = tuple(step for _, step in halves)
    return pl.pallas_call(
        functools.partial(total_kernel, (len(nears), steps)),
        out_shape=jax.ShapeDtypeStruct(nears[0].shape, F32),
        in_specs=[SMEM] + [VMEM] * (1 + len(nears) + len(arrays)),
        out_specs=VMEM,
        compiler_params=params(size_of(*nears, nears[0], incident, *arrays)),
        name="total",
    )(side, incident, *nears, *arrays)


def from_other(value):
    return lax.ppermute(value, "pair", [(0, 1), (1, 0)])


def across(value, bit):
    count = lax.axis_size("owner")
    return lax.ppermute(value, "owner", [(source, source ^ bit) for source in range(count)])


def scatter_step(incident, scattered, blocks, parts, index, side, layers):
    particles = incident.shape[0]
    every = range(particles)
    by_x = range((particles + 1) // 2)
    by_y = range((particles + 1) // 2, particles)
    rest = range(1, layers)
    powers = [1 << step for step in range(layers.bit_length() - 1)]
    at = functools.partial(place_of, particles=particles, layers=layers)
    total_rows = COLUMNS * particles * layers
    first_n, first_d = at(1, 0, 0), at(3, 0, 0)
    first = parts is None

    def row_of(particle, layer):
        return particle * layers + layer

    other = from_other(scattered)
    x1 = across(scattered, 1)
    y1 = across(scattered, 2)
    reached = [across(scattered, COLUMNS)]
    where = {1: (0, 0), 2: (1, 0), 3: (2, 0)}
    fetched = (scattered, other, blocks)
    products_d, *made = backward(
        first, (2, 4), first_d, total_rows - first_d, index, *fetched, parts
    )
    if first:
        parts = made[0]

    inputs = [products_d, x1, y1, scattered]
    x_plan = [[(0, row_of(particle, layer))] for particle in by_x for layer in range(layers)]
    y_plan = [[(0, row_of(particle, layer))] for particle in by_y for layer in range(layers)]
    x_head, y_head = len(x_plan), len(y_plan)
    x_plan += [[(2, particle)] for particle in by_y]
    y_plan += [[(1, particle)] for particle in by_x]
    x2, y2, copied = pack(
        "pack_second",
        inputs,
        [x_plan, y_plan, [[(3, particle)] for particle in every]],
        reached,
    )
    x2, y2 = across(x2, 1), across(y2, 2)
    reached.append(across(copied, 2 * COLUMNS))
    products_n, *made = backward(first, (1, 3), first_n, first_d - first_n, index, *fetched, parts)
    if first:
        parts = made[0]

    def z_row(particle, layer):
        number, start = where[layer]
        return number, start + particle

    inputs = [products_n, x2, y2, scattered, reached[0]]
    x_plan, y_plan = [], []
    for particle in every:
        for layer in range(layers):
            x_terms = [(0, at(1, particle, layer) - first_n)]
            y_terms = [(0, at(2, particle, layer) - first_n)]
            if particle in by_x:
                y_terms.append((1, row_of(particle, layer)))
            else:
                x_terms.append((2, row_of(particle - len(by_x), layer)))
            x_plan.append(x_terms)
            y_plan.append(y_terms)
    z_plans = [[[(number, particle)] for particle in every] for number in (3, 4)]
    x3, y3, copied, known = pack("pack_third", inputs, [x_plan, y_plan] + z_plans, reached[1:])
    x3, y3 = across(x3, 1), across(y3, 2)
    reached.append(across(known, 2 * COLUMNS))
    for bit in powers[2:]:
        plan = [[(0, particle)] for particle in every]
        for layer in range(1, bit):
            plan += [[(1 + where[layer][0], where[layer][1] + particle)] for particle in every]
        (known,) = pack("pack_layers", [scattered] + reached, [plan])
        for layer in range(bit):
            where[bit + layer] = (len(reached), layer * particles)
        reached.append(across(known, bit * COLUMNS))
    products_o, *made = backward(first, (0,), 0, first_n, index, copied, other, blocks, parts)
    if first:
        parts = made[0]
    copies = []
    for particle in every:
        copies.append((0, particle, at(1, particle, 0)))
        copies.append((1, particle, at(2, particle, 0)))
        if particle in by_x:
            copies.append((3, y_head + particle, at(3, particle, 0)))
        else:
            copies.append((2, x_head + particle - len(by_x), at(3, particle, 0)))
    sizes = (particles, total_rows)
    near = forward(
        (1, 2), index, [x1, y1, x2, y2], tuple(copies), parts, *sizes, None, False, [products_o]
    )

    def summed(layer, particle, arrived):
        terms = [(number, row_of(particle, layer)) for number in range(3)]
        for step in range(arrived):
            terms.append((3 + step, (layer >> (step + 1)) * particles + particle))
        return terms

    def half_sums(bit, arrived):
        chosen = range(bit, layers, 2 * bit)
        return [summed(layer, particle, arrived) for layer in chosen for particle in every]

    inputs = [products_o, x3, y3] + reached
    tails = []
    for particle in every:
        for layer in rest:
            step, row = z_row(particle, layer)
            tails.append([(3 + step, row)])
    x4, y4, sums, mark = pack(
        "pack_fourth",
        inputs,
        [tails, tails, half_sums(1, 0), [[(1, 0)]]],
        [near],
    )
    x4, y4 = across(x4, 1), across(y4, 2)
    arrived = [across(sums, COLUMNS)]
    copies = []
    for particle in every:
        for layer in rest:
            step, row = z_row(particle, layer)
            copies.append((step, row, at(0, particle, layer)))
    near = forward((0,), index, reached, tuple(copies), parts, *sizes, near, False, [mark])

    def tail(particle, layer):
        return particle * len(rest) + layer - 1

    x5, y5, mark = pack(
        "pack_fifth",
        [x4, y4],
        [
            [[(1, tail(particle, layer))] for particle in by_y for layer in rest],
            [[(0, tail(particle, layer))] for particle in by_x for layer in rest],
            [[(0, 0)]],
        ],
        [near],
    )
    x5, y5 = across(x5, 1), across(y5, 2)
    for bit in powers[1:]:
        inputs = [products_o, x3, y3] + arrived
        (sums,) = pack("pack_sums", inputs, [half_sums(bit, len(arrived))], [mark])
        arrived.append(across(sums, bit * COLUMNS))
    copies = []
    for particle in every:
        for layer in rest:
            copies.append((0, tail(particle, layer), at(1, particle, layer)))
            copies.append((1, tail(particle, layer), at(2, particle, layer)))
    near = forward((3,), index, [x4, y4], tuple(copies), parts, *sizes, near, False, [mark, sums])
    copies = []
    for number, group in ((0, by_y), (1, by_x)):
        for order, particle in enumerate(group):
            for layer in rest:
                copies.append((number, tail(order, layer), at(3, particle, layer)))
    near = forward((4,), index, [x5, y5], tuple(copies), parts, *sizes, near, True, [])
    halves = [(products_o, layers), (x3, layers), (y3, layers)] + [(value, 1) for value in arrived]
    return whole_total(side, incident, [near], halves), parts


def local(incident, tmat, blocks, block_rows, partners, live, owner_of):
    layers = lax.axis_size("owner") // COLUMNS
    my_owner = lax.axis_index("owner").astype(jnp.int32)[None]
    side = lax.axis_index("pair").astype(jnp.int32)[None]
    theirs = from_other(incident)
    index = slot_index(
        my_owner, side, partners, owner_of, block_rows, live, layers, incident.shape[0]
    )
    tmat_parts, incident = prepare(tmat, incident, index)
    (scattered,) = apply_tmat(True, False, side, incident, theirs, tmat_parts)
    parts = None
    for turn in range(ITERS):
        mine, parts = scatter_step(incident, scattered, blocks, parts, index, side, layers)
        theirs = from_other(mine)
        last = turn == ITERS - 1
        *exciting, scattered = apply_tmat(False, last, side, mine, theirs, tmat_parts)
    return (scattered, exciting[0])


def solution(mesh):
    in_specs = (
        P("owner", None, None, "pair"),
        P("owner", None, "pair", None),
        P("owner", None, None, "pair"),
        P("owner"),
        P(),
        P("owner"),
        P(),
    )
    out_specs = (P("owner", None, None, "pair"), P("owner", None, None, "pair"))
    return jax.shard_map(local, mesh=mesh, in_specs=in_specs, out_specs=out_specs, check_vma=False)
```

profile of v0, /device:TPU:0, one launch (start us, length us, event | category | flops | bytes accessed | tf_op | source)
XLA Modules:
  0.0 126.1 jit_solution(5287091165409161682)
XLA Ops:
  1.8 1.7 %slot_index.1.after_ref.index_ref = s32[321]{0:T(512)} custom-call(s32[1]{0:T(128)} %bitcast.1.owner_ref, s32[1]{0:T(128)} %bitcast.side_ref, s32[336]{0:T(512)} %partners_ref.1, s32[32]{0:T(128)} %rows_of_ref.1, s32[21]{0:T(128)} %holders_ref.1, s32[1]{0:T(128)S(6)} %copy.13.live_ref), custom_call_target="tpu_custom_call" | custom-call | tf_op jit(solution)/shard_map/slot_index/pallas_call | solution.py:92
  3.5 1.6 %copy-done = f32[2,2,256,512]{3,2,1,0:T(8,128)S(1)} copy-done((f32[2,2,256,512]{3,2,1,0:T(8,128)S(1)}, f32[2,2,256,512]{3,2,1,0:T(8,128)}, u32[]{:S(2)}) %copy-start) | copy-done | bytes 2097176
  8.4 3.2 %collective-permute-start.4 = (f32[2,2,32,256]{3,2,1,0:T(8,128)S(1)}, f32[2,2,32,256]{3,2,1,0:T(8,128)S(1)}, u32[]{:S(2)}, u32[]{:S(2)}) collective-permute-start(f32[2,2,32,256]{3,2,1,0:T(8,128)S(1)} %tmat_apply.3.own_ref.refs_3_), channel_id=1, source_target_pairs={{0,8},{2,10},{4,12},{6,14},{8,0},{10,2},{12,4},{14,6},{16,24},{18,... | collective-permute-start | bytes 393224 | tf_op jit(solution)/shard_map/ppermute | solution.py:451
  15.0 4.5 %backward_group2.2 = (f32[8,2,32,256]{3,2,1,0:T(8,128)S(1)}, bf16[21,2,2,512,256]{4,3,2,1,0:T(8,128)(2,1)}) custom-call(s32[321]{0:T(512)S(1)} %copy-done.2, f32[2,2,32,256]{3,2,1,0:T(8,128)S(1)} %tmat_apply.3.own_ref.refs_3_, f32[2,2,32,256]{3,2,1,0:T(8,128)S(1)} %collective-permute-done.1.other_ref, f32[21,2,512,256]{3,2,1,0:T(8,128)} %blocks_ref.5), custom_call_target="tpu_custom_call" | custom-call | flops 4194304 | bytes 131072 | tf_op jit(solution)/shard_map/backward_group2/pallas_call | solution.py:300
  20.2 2.9 %collective-permute-start.7 = (f32[2,2,32,256]{3,2,1,0:T(8,128)S(1)}, f32[2,2,32,256]{3,2,1,0:T(8,128)S(1)}, u32[]{:S(2)}, u32[]{:S(2)}) collective-permute-start(f32[2,2,32,256]{3,2,1,0:T(8,128)S(1)} %get-tuple-element.47), channel_id=1, source_target_pairs={{0,16},{2,18},{4,20},{6,22},{8,24},{10,26},{12,28},{14,30},{16,0},... | collective-permute-start | bytes 393224 | tf_op jit(solution)/shard_map/ppermute | solution.py:451
  23.1 6.8 %backward_group1.2 = (f32[16,2,32,256]{3,2,1,0:T(8,128)S(1)}, bf16[21,2,2,512,256]{4,3,2,1,0:T(8,128)(2,1)}) custom-call(s32[321]{0:T(512)S(1)} %copy-done.2, f32[2,2,32,256]{3,2,1,0:T(8,128)S(1)} %tmat_apply.3.own_ref.refs_3_, f32[2,2,32,256]{3,2,1,0:T(8,128)S(1)} %collective-permute-done.1.other_ref, ...), custom_call_target="tpu_custom_call", output_to_operand_aliasing={{1}: (4, {})} | custom-call | flops 4194304 | bytes 131072 | tf_op jit(solution)/shard_map/backward_group1/pallas_call | solution.py:300
  31.2 3.0 %collective-permute-start.9 = (f32[8,2,32,256]{3,2,1,0:T(8,128)S(1)}, f32[8,2,32,256]{3,2,1,0:T(8,128)S(1)}, u32[]{:S(2)}, u32[]{:S(2)}) collective-permute-start(f32[8,2,32,256]{3,2,1,0:T(8,128)S(1)} %get-tuple-element.52), channel_id=1, source_target_pairs={{0,4},{2,6},{4,0},{6,2},{8,12},{10,14},{12,8},{14,10},{16,20},{18,... | collective-permute-start | bytes 1572872 | tf_op jit(solution)/shard_map/ppermute | solution.py:451
  34.2 2.3 %collective-permute-start.10 = (f32[2,2,32,256]{3,2,1,0:T(8,128)S(1)}, f32[2,2,32,256]{3,2,1,0:T(8,128)S(1)}, u32[]{:S(2)}, u32[]{:S(2)}) collective-permute-start(f32[2,2,32,256]{3,2,1,0:T(8,128)S(1)} %get-tuple-element.53), channel_id=1, source_target_pairs={{0,16},{2,18},{4,20},{6,22},{8,24},{10,26},{12,28},{14,30},{16,0},... | collective-permute-start | bytes 393224 | tf_op jit(solution)/shard_map/ppermute | solution.py:451
  36.5 4.2 %backward_group0.2 = (f32[8,2,32,256]{3,2,1,0:T(8,128)S(1)}, bf16[21,2,2,512,256]{4,3,2,1,0:T(8,128)(2,1)}) custom-call(s32[321]{0:T(512)S(1)} %copy-done.2, f32[2,2,32,256]{3,2,1,0:T(8,128)S(1)} %get-tuple-element.48.own_ref, f32[2,2,32,256]{3,2,1,0:T(8,128)S(1)} %collective-permute-done.1.other_ref, ...), custom_call_target="tpu_custom_call", output_to_operand_aliasing={{1}: (4, {})} | custom-call | flops 4194304 | bytes 131072 | tf_op jit(solution)/shard_map/backward_group0/pallas_call | solution.py:300
  40.7 3.2 %forward_group1.2.refs_6_.refs_4_ = f32[2,512,128]{2,1,0:T(8,128)S(1)} custom-call(s32[321]{0:T(512)S(1)} %copy-done.2, f32[2,2,32,256]{3,2,1,0:T(8,128)S(1)} %collective-permute-done.2.refs_1_.refs_0_, f32[2,2,32,256]{3,2,1,0:T(8,128)S(1)} %collective-permute-done.3.refs_2_.refs_1_, f32[5,2,32,256]{3,2,1,0:T(8,128)S(1)} %collective-permute-done.5.refs_1_.refs_2_, ...), custom_call_target="tpu_custom_call" | custom-call | flops 4194304 | bytes 524288 | tf_op jit(solution)/shard_map/forward_group1/pallas_call | solution.py:378
  44.1 1.7 %collective-permute-start.11 = (f32[6,2,32,256]{3,2,1,0:T(8,128)S(1)}, f32[6,2,32,256]{3,2,1,0:T(8,128)S(1)}, u32[]{:S(2)}, u32[]{:S(2)}) collective-permute-start(f32[6,2,32,256]{3,2,1,0:T(8,128)S(1)} %get-tuple-element.55), channel_id=1, source_target_pairs={{0,2},{2,0},{4,6},{6,4},{8,10},{10,8},{12,14},{14,12},{16,18},{18,... | collective-permute-start | bytes 1179656 | tf_op jit(solution)/shard_map/ppermute | solution.py:451
  45.8 1.7 %collective-permute-start.12 = (f32[6,2,32,256]{3,2,1,0:T(8,128)S(1)}, f32[6,2,32,256]{3,2,1,0:T(8,128)S(1)}, u32[]{:S(2)}, u32[]{:S(2)}) collective-permute-start(f32[6,2,32,256]{3,2,1,0:T(8,128)S(1)} %get-tuple-element.56), channel_id=1, source_target_pairs={{0,4},{2,6},{4,0},{6,2},{8,12},{10,14},{12,8},{14,10},{16,20},{18,... | collective-permute-start | bytes 1179656 | tf_op jit(solution)/shard_map/ppermute | solution.py:451
  48.9 3.2 %forward_group0.2.refs_2_.refs_3_ = f32[2,512,128]{2,1,0:T(8,128)S(1)} custom-call(s32[321]{0:T(512)S(1)} %copy-done.2, f32[2,2,32,256]{3,2,1,0:T(8,128)S(1)} %collective-permute-done.4.refs_4_.refs_3_.refs_0_, f32[2,2,32,256]{3,2,1,0:T(8,128)S(1)} %collective-permute-done.7.refs_5_.refs_4_.refs_1_, ...), custom_call_target="tpu_custom_call" | custom-call | flops 4194304 | bytes 524288 | tf_op jit(solution)/shard_map/forward_group0/pallas_call | solution.py:378
  53.7 1.7 %collective-permute-start.13 = (f32[3,2,32,256]{3,2,1,0:T(8,128)S(1)}, f32[3,2,32,256]{3,2,1,0:T(8,128)S(1)}, u32[]{:S(2)}, u32[]{:S(2)}) collective-permute-start(f32[3,2,32,256]{3,2,1,0:T(8,128)S(1)} %get-tuple-element.58), channel_id=1, source_target_pairs={{0,2},{2,0},{4,6},{6,4},{8,10},{10,8},{12,14},{14,12},{16,18},{18,... | collective-permute-start | bytes 589832 | tf_op jit(solution)/shard_map/ppermute | solution.py:451
  55.3 1.7 %collective-permute-start.14 = (f32[3,2,32,256]{3,2,1,0:T(8,128)S(1)}, f32[3,2,32,256]{3,2,1,0:T(8,128)S(1)}, u32[]{:S(2)}, u32[]{:S(2)}) collective-permute-start(f32[3,2,32,256]{3,2,1,0:T(8,128)S(1)} %get-tuple-element.59), channel_id=1, source_target_pairs={{0,4},{2,6},{4,0},{6,2},{8,12},{10,14},{12,8},{14,10},{16,20},{18,... | collective-permute-start | bytes 589832 | tf_op jit(solution)/shard_map/ppermute | solution.py:451
  57.1 2.2 %collective-permute-start.16 = (f32[2,2,32,256]{3,2,1,0:T(8,128)S(1)}, f32[2,2,32,256]{3,2,1,0:T(8,128)S(1)}, u32[]{:S(2)}, u32[]{:S(2)}) collective-permute-start(f32[2,2,32,256]{3,2,1,0:T(8,128)S(1)} %pack_sums.2.refs_5_), channel_id=1, source_target_pairs={{0,16},{2,18},{4,20},{6,22},{8,24},{10,26},{12,28},{14,30},{16,0},... | collective-permute-start | bytes 393224 | tf_op jit(solution)/shard_map/ppermute | solution.py:451
  59.3 4.5 %forward_group3.2.refs_3_ = f32[2,512,128]{2,1,0:T(8,128)S(1)} custom-call(s32[321]{0:T(512)S(1)} %copy-done.2, f32[6,2,32,256]{3,2,1,0:T(8,128)S(1)} %collective-permute-done.11.refs_0_, f32[6,2,32,256]{3,2,1,0:T(8,128)S(1)} %collective-permute-done.12.refs_1_, bf16[21,2,2,512,256]{4,3,2,1,0:T(8,128)(2,1)} %get-tuple-element.54.refs_4_.refs_3_.refs_2_.blocks_ref, ...), custom_call_target="tpu_custom_call" | custom-call | flops 4194304 | bytes 524288 | tf_op jit(solution)/shard_map/forward_group3/pallas_call | solution.py:378
  63.9 3.0 %forward_group4.2.refs_0_ = f32[2,2,32,512]{3,2,1,0:T(8,128)S(1)} custom-call(s32[321]{0:T(512)S(1)} %copy-done.2, f32[3,2,32,256]{3,2,1,0:T(8,128)S(1)} %collective-permute-done.13.refs_0_, f32[3,2,32,256]{3,2,1,0:T(8,128)S(1)} %collective-permute-done.14.refs_1_, bf16[21,2,2,512,256]{4,3,2,1,0:T(8,128)(2,1)} %get-tuple-element.54.refs_4_.refs_3_.refs_2_.blocks_ref, ...), custom_call_target="tpu_custom_call" | custom-call | flops 4194304 | bytes 262144 | tf_op jit(solution)/shard_map/forward_group4/pallas_call | solution.py:378
  67.1 1.5 %collective-permute-done.17.theirs_ref = f32[2,2,32,512]{3,2,1,0:T(8,128)S(1)} collective-permute-done((f32[2,2,32,512]{3,2,1,0:T(8,128)S(1)}, f32[2,2,32,512]{3,2,1,0:T(8,128)S(1)}, u32[]{:S(2)}, u32[]{:S(2)}) %collective-permute-start.17) | collective-permute-done | bytes 262176 | tf_op jit(solution)/shard_map/ppermute | solution.py:446
  69.7 3.0 %collective-permute-start.21 = (f32[2,2,32,256]{3,2,1,0:T(8,128)S(1)}, f32[2,2,32,256]{3,2,1,0:T(8,128)S(1)}, u32[]{:S(2)}, u32[]{:S(2)}) collective-permute-start(f32[2,2,32,256]{3,2,1,0:T(8,128)S(1)} %tmat_apply.4.own_ref.refs_3_), channel_id=1, source_target_pairs={{0,8},{2,10},{4,12},{6,14},{8,0},{10,2},{12,4},{14,6},{16,24},{18,... | collective-permute-start | bytes 393224 | tf_op jit(solution)/shard_map/ppermute | solution.py:451
  74.0 3.1 %backward_group2.3.refs_0_ = f32[8,2,32,256]{3,2,1,0:T(8,128)S(1)} custom-call(s32[321]{0:T(512)S(1)} %copy-done.2, f32[2,2,32,256]{3,2,1,0:T(8,128)S(1)} %tmat_apply.4.own_ref.refs_3_, f32[2,2,32,256]{3,2,1,0:T(8,128)S(1)} %collective-permute-done.18.other_ref, bf16[21,2,2,512,256]{4,3,2,1,0:T(8,128)(2,1)} %get-tuple-element.54.refs_4_.refs_3_.refs_2_.blocks_ref), custom_call_target="tpu_custom_call" | custom-call | flops 4194304 | bytes 131072 | tf_op jit(solution)/shard_map/backward_group2/pallas_call | solution.py:300
  80.3 1.7 %collective-permute-start.24 = (f32[2,2,32,256]{3,2,1,0:T(8,128)S(1)}, f32[2,2,32,256]{3,2,1,0:T(8,128)S(1)}, u32[]{:S(2)}, u32[]{:S(2)}) collective-permute-start(f32[2,2,32,256]{3,2,1,0:T(8,128)S(1)} %get-tuple-element.64), channel_id=1, source_target_pairs={{0,16},{2,18},{4,20},{6,22},{8,24},{10,26},{12,28},{14,30},{16,0},... | collective-permute-start | bytes 393224 | tf_op jit(solution)/shard_map/ppermute | solution.py:451
  82.0 4.3 %backward_group1.3.refs_0_ = f32[16,2,32,256]{3,2,1,0:T(8,128)S(1)} custom-call(s32[321]{0:T(512)S(1)} %copy-done.2, f32[2,2,32,256]{3,2,1,0:T(8,128)S(1)} %tmat_apply.4.own_ref.refs_3_, f32[2,2,32,256]{3,2,1,0:T(8,128)S(1)} %collective-permute-done.18.other_ref, bf16[21,2,2,512,256]{4,3,2,1,0:T(8,128)(2,1)} %get-tuple-element.54.refs_4_.refs_3_.refs_2_.blocks_ref), custom_call_target="tpu_custom_call" | custom-call | flops 4194304 | bytes 131072 | tf_op jit(solution)/shard_map/backward_group1/pallas_call | solution.py:300
  86.3 1.7 %collective-permute-done.24.refs_5_.refs_4_.refs_1_ = f32[2,2,32,256]{3,2,1,0:T(8,128)S(1)} collective-permute-done((f32[2,2,32,256]{3,2,1,0:T(8,128)S(1)}, f32[2,2,32,256]{3,2,1,0:T(8,128)S(1)}, u32[]{:S(2)}, u32[]{:S(2)}) %collective-permute-start.24) | collective-permute-done | bytes 131104 | tf_op jit(solution)/shard_map/ppermute | solution.py:451
  92.4 2.7 %backward_group0.3.refs_5_.refs_0_.refs_1_ = f32[8,2,32,256]{3,2,1,0:T(8,128)S(1)} custom-call(s32[321]{0:T(512)S(1)} %copy-done.2, f32[2,2,32,256]{3,2,1,0:T(8,128)S(1)} %get-tuple-element.65.own_ref, f32[2,2,32,256]{3,2,1,0:T(8,128)S(1)} %collective-permute-done.18.other_ref, bf16[21,2,2,512,256]{4,3,2,1,0:T(8,128)(2,1)} %get-tuple-element.54.refs_4_.refs_3_.refs_2_.blocks_ref), custom_call_target="tpu_custom_call" | custom-call | flops 4194304 | bytes 131072 | tf_op jit(solution)/shard_map/backward_group0/pallas_call | solution.py:300
  95.1 3.2 %forward_group1.3.refs_6_.refs_4_ = f32[2,512,128]{2,1,0:T(8,128)S(1)} custom-call(s32[321]{0:T(512)S(1)} %copy-done.2, f32[2,2,32,256]{3,2,1,0:T(8,128)S(1)} %collective-permute-done.19.refs_1_.refs_0_, f32[2,2,32,256]{3,2,1,0:T(8,128)S(1)} %collective-permute-done.20.refs_2_.refs_1_, f32[5,2,32,256]{3,2,1,0:T(8,128)S(1)} %collective-permute-done.22.refs_1_.refs_2_, ...), custom_call_target="tpu_custom_call" | custom-call | flops 4194304 | bytes 524288 | tf_op jit(solution)/shard_map/forward_group1/pallas_call | solution.py:378
  98.3 3.1 %collective-permute-done.25.refs_1_.refs_2_ = f32[8,2,32,256]{3,2,1,0:T(8,128)S(1)} collective-permute-done((f32[8,2,32,256]{3,2,1,0:T(8,128)S(1)}, f32[8,2,32,256]{3,2,1,0:T(8,128)S(1)}, u32[]{:S(2)}, u32[]{:S(2)}) %collective-permute-start.25) | collective-permute-done | bytes 524320 | tf_op jit(solution)/shard_map/ppermute | solution.py:451
  104.8 3.2 %forward_group0.3.refs_2_.refs_3_ = f32[2,512,128]{2,1,0:T(8,128)S(1)} custom-call(s32[321]{0:T(512)S(1)} %copy-done.2, f32[2,2,32,256]{3,2,1,0:T(8,128)S(1)} %collective-permute-done.21.refs_4_.refs_3_.refs_0_, f32[2,2,32,256]{3,2,1,0:T(8,128)S(1)} %collective-permute-done.24.refs_5_.refs_4_.refs_1_, ...), custom_call_target="tpu_custom_call" | custom-call | flops 4194304 | bytes 524288 | tf_op jit(solution)/shard_map/forward_group0/pallas_call | solution.py:378
  107.9 3.2 %collective-permute-done.28.refs_0_ = f32[6,2,32,256]{3,2,1,0:T(8,128)S(1)} collective-permute-done((f32[6,2,32,256]{3,2,1,0:T(8,128)S(1)}, f32[6,2,32,256]{3,2,1,0:T(8,128)S(1)}, u32[]{:S(2)}, u32[]{:S(2)}) %collective-permute-start.28) | collective-permute-done | bytes 393248 | tf_op jit(solution)/shard_map/ppermute | solution.py:451
  115.3 4.5 %forward_group3.3.refs_3_ = f32[2,512,128]{2,1,0:T(8,128)S(1)} custom-call(s32[321]{0:T(512)S(1)} %copy-done.2, f32[6,2,32,256]{3,2,1,0:T(8,128)S(1)} %collective-permute-done.28.refs_0_, f32[6,2,32,256]{3,2,1,0:T(8,128)S(1)} %collective-permute-done.29.refs_1_, bf16[21,2,2,512,256]{4,3,2,1,0:T(8,128)(2,1)} %get-tuple-element.54.refs_4_.refs_3_.refs_2_.blocks_ref, ...), custom_call_target="tpu_custom_call" | custom-call | flops 4194304 | bytes 524288 | tf_op jit(solution)/shard_map/forward_group3/pallas_call | solution.py:378
  119.8 3.0 %forward_group4.3.refs_0_ = f32[2,2,32,512]{3,2,1,0:T(8,128)S(1)} custom-call(s32[321]{0:T(512)S(1)} %copy-done.2, f32[3,2,32,256]{3,2,1,0:T(8,128)S(1)} %collective-permute-done.30.refs_0_, f32[3,2,32,256]{3,2,1,0:T(8,128)S(1)} %collective-permute-done.31.refs_1_, bf16[21,2,2,512,256]{4,3,2,1,0:T(8,128)(2,1)} %get-tuple-element.54.refs_4_.refs_3_.refs_2_.blocks_ref, ...), custom_call_target="tpu_custom_call" | custom-call | flops 4194304 | bytes 262144 | tf_op jit(solution)/shard_map/forward_group4/pallas_call | solution.py:378
  124.5 1.5 %tmat_apply.5 = (f32[2,2,32,256]{3,2,1,0:T(8,128)}, f32[2,2,32,256]{3,2,1,0:T(8,128)}) custom-call(s32[1]{0:T(128)} %bitcast.side_ref, f32[2,2,32,512]{3,2,1,0:T(8,128)S(1)} %total.3.mine_ref, f32[2,2,32,512]{3,2,1,0:T(8,128)S(1)} %collective-permute-done.34.theirs_ref, bf16[2,256,2048]{2,1,0:T(8,128)(2,1)S(1)} %get-tuple-element.41.parts_ref), custom_call_target="tpu_custom_call" | custom-call | tf_op jit(solution)/shard_map/tmat_apply/pallas_call | solution.py:171
  (77 shorter events, 31.4 us)
Async XLA Ops:
  0.6 6.7 %collective-permute-start = (f32[2,2,32,256]{3,2,1,0:T(8,128)}, f32[2,2,32,256]{3,2,1,0:T(8,128)S(1)}, u32[]{:S(2)}, u32[]{:S(2)}) collective-permute-start(f32[2,2,32,256]{3,2,1,0:T(8,128)} %incident_ref.1), channel_id=1, source_target_pairs={{0,1},{1,0},{2,3},{3,2},{4,5},{5,4},{6,7},{7,6},{8,9},{9,8},{10,11... | collective-permute-start | bytes 393224 | tf_op jit(solution)/shard_map/ppermute | solution.py:446
  8.3 6.1 %collective-permute-start.1 = (f32[2,2,32,256]{3,2,1,0:T(8,128)S(1)}, f32[2,2,32,256]{3,2,1,0:T(8,128)S(1)}, u32[]{:S(2)}, u32[]{:S(2)}) collective-permute-start(f32[2,2,32,256]{3,2,1,0:T(8,128)S(1)} %tmat_apply.3.own_ref.refs_3_), channel_id=1, source_target_pairs={{0,1},{1,0},{2,3},{3,2},{4,5},{5,4},{6,7},{7,6},{8,9},{9,8},{10,11... | collective-permute-start | bytes 393224 | tf_op jit(solution)/shard_map/ppermute | solution.py:446
  8.4 11.2 %collective-permute-start.4 = (f32[2,2,32,256]{3,2,1,0:T(8,128)S(1)}, f32[2,2,32,256]{3,2,1,0:T(8,128)S(1)}, u32[]{:S(2)}, u32[]{:S(2)}) collective-permute-start(f32[2,2,32,256]{3,2,1,0:T(8,128)S(1)} %tmat_apply.3.own_ref.refs_3_), channel_id=1, source_target_pairs={{0,8},{2,10},{4,12},{6,14},{8,0},{10,2},{12,4},{14,6},{16,24},{18,... | collective-permute-start | bytes 393224 | tf_op jit(solution)/shard_map/ppermute | solution.py:451
  11.6 7.9 %collective-permute-start.3 = (f32[2,2,32,256]{3,2,1,0:T(8,128)S(1)}, f32[2,2,32,256]{3,2,1,0:T(8,128)S(1)}, u32[]{:S(2)}, u32[]{:S(2)}) collective-permute-start(f32[2,2,32,256]{3,2,1,0:T(8,128)S(1)} %tmat_apply.3.own_ref.refs_3_), channel_id=1, source_target_pairs={{0,4},{2,6},{4,0},{6,2},{8,12},{10,14},{12,8},{14,10},{16,20},{18,... | collective-permute-start | bytes 393224 | tf_op jit(solution)/shard_map/ppermute | solution.py:451
  13.1 6.5 %collective-permute-start.2 = (f32[2,2,32,256]{3,2,1,0:T(8,128)S(1)}, f32[2,2,32,256]{3,2,1,0:T(8,128)S(1)}, u32[]{:S(2)}, u32[]{:S(2)}) collective-permute-start(f32[2,2,32,256]{3,2,1,0:T(8,128)S(1)} %tmat_apply.3.own_ref.refs_3_), channel_id=1, source_target_pairs={{0,2},{2,0},{4,6},{6,4},{8,10},{10,8},{12,14},{14,12},{16,18},{18,... | collective-permute-start | bytes 393224 | tf_op jit(solution)/shard_map/ppermute | solution.py:451
  19.6 10.3 %collective-permute-start.5 = (f32[5,2,32,256]{3,2,1,0:T(8,128)S(1)}, f32[5,2,32,256]{3,2,1,0:T(8,128)S(1)}, u32[]{:S(2)}, u32[]{:S(2)}) collective-permute-start(f32[5,2,32,256]{3,2,1,0:T(8,128)S(1)} %get-tuple-element.45), channel_id=1, source_target_pairs={{0,2},{2,0},{4,6},{6,4},{8,10},{10,8},{12,14},{14,12},{16,18},{18,... | collective-permute-start | bytes 983048 | tf_op jit(solution)/shard_map/ppermute | solution.py:451
  19.7 10.3 %collective-permute-start.6 = (f32[5,2,32,256]{3,2,1,0:T(8,128)S(1)}, f32[5,2,32,256]{3,2,1,0:T(8,128)S(1)}, u32[]{:S(2)}, u32[]{:S(2)}) collective-permute-start(f32[5,2,32,256]{3,2,1,0:T(8,128)S(1)} %get-tuple-element.46), channel_id=1, source_target_pairs={{0,4},{2,6},{4,0},{6,2},{8,12},{10,14},{12,8},{14,10},{16,20},{18,... | collective-permute-start | bytes 983048 | tf_op jit(solution)/shard_map/ppermute | solution.py:451
  20.2 9.8 %collective-permute-start.7 = (f32[2,2,32,256]{3,2,1,0:T(8,128)S(1)}, f32[2,2,32,256]{3,2,1,0:T(8,128)S(1)}, u32[]{:S(2)}, u32[]{:S(2)}) collective-permute-start(f32[2,2,32,256]{3,2,1,0:T(8,128)S(1)} %get-tuple-element.47), channel_id=1, source_target_pairs={{0,16},{2,18},{4,20},{6,22},{8,24},{10,26},{12,28},{14,30},{16,0},... | collective-permute-start | bytes 393224 | tf_op jit(solution)/shard_map/ppermute | solution.py:451
  30.1 13.8 %collective-permute-start.8 = (f32[8,2,32,256]{3,2,1,0:T(8,128)S(1)}, f32[8,2,32,256]{3,2,1,0:T(8,128)S(1)}, u32[]{:S(2)}, u32[]{:S(2)}) collective-permute-start(f32[8,2,32,256]{3,2,1,0:T(8,128)S(1)} %get-tuple-element.51), channel_id=1, source_target_pairs={{0,2},{2,0},{4,6},{6,4},{8,10},{10,8},{12,14},{14,12},{16,18},{18,... | collective-permute-start | bytes 1572872 | tf_op jit(solution)/shard_map/ppermute | solution.py:451
  31.2 12.9 %collective-permute-start.9 = (f32[8,2,32,256]{3,2,1,0:T(8,128)S(1)}, f32[8,2,32,256]{3,2,1,0:T(8,128)S(1)}, u32[]{:S(2)}, u32[]{:S(2)}) collective-permute-start(f32[8,2,32,256]{3,2,1,0:T(8,128)S(1)} %get-tuple-element.52), channel_id=1, source_target_pairs={{0,4},{2,6},{4,0},{6,2},{8,12},{10,14},{12,8},{14,10},{16,20},{18,... | collective-permute-start | bytes 1572872 | tf_op jit(solution)/shard_map/ppermute | solution.py:451
  34.2 9.7 %collective-permute-start.10 = (f32[2,2,32,256]{3,2,1,0:T(8,128)S(1)}, f32[2,2,32,256]{3,2,1,0:T(8,128)S(1)}, u32[]{:S(2)}, u32[]{:S(2)}) collective-permute-start(f32[2,2,32,256]{3,2,1,0:T(8,128)S(1)} %get-tuple-element.53), channel_id=1, source_target_pairs={{0,16},{2,18},{4,20},{6,22},{8,24},{10,26},{12,28},{14,30},{16,0},... | collective-permute-start | bytes 393224 | tf_op jit(solution)/shard_map/ppermute | solution.py:451
  44.1 8.5 %collective-permute-start.11 = (f32[6,2,32,256]{3,2,1,0:T(8,128)S(1)}, f32[6,2,32,256]{3,2,1,0:T(8,128)S(1)}, u32[]{:S(2)}, u32[]{:S(2)}) collective-permute-start(f32[6,2,32,256]{3,2,1,0:T(8,128)S(1)} %get-tuple-element.55), channel_id=1, source_target_pairs={{0,2},{2,0},{4,6},{6,4},{8,10},{10,8},{12,14},{14,12},{16,18},{18,... | collective-permute-start | bytes 1179656 | tf_op jit(solution)/shard_map/ppermute | solution.py:451
  45.8 7.8 %collective-permute-start.12 = (f32[6,2,32,256]{3,2,1,0:T(8,128)S(1)}, f32[6,2,32,256]{3,2,1,0:T(8,128)S(1)}, u32[]{:S(2)}, u32[]{:S(2)}) collective-permute-start(f32[6,2,32,256]{3,2,1,0:T(8,128)S(1)} %get-tuple-element.56), channel_id=1, source_target_pairs={{0,4},{2,6},{4,0},{6,2},{8,12},{10,14},{12,8},{14,10},{16,20},{18,... | collective-permute-start | bytes 1179656 | tf_op jit(solution)/shard_map/ppermute | solution.py:451
  47.6 9.5 %collective-permute-start.15 = (f32[4,2,32,256]{3,2,1,0:T(8,128)S(1)}, f32[4,2,32,256]{3,2,1,0:T(8,128)S(1)}, u32[]{:S(2)}, u32[]{:S(2)}) collective-permute-start(f32[4,2,32,256]{3,2,1,0:T(8,128)S(1)} %get-tuple-element.61), channel_id=1, source_target_pairs={{0,8},{2,10},{4,12},{6,14},{8,0},{10,2},{12,4},{14,6},{16,24},{18,... | collective-permute-start | bytes 786440 | tf_op jit(solution)/shard_map/ppermute | solution.py:451
  53.7 10.2 %collective-permute-start.13 = (f32[3,2,32,256]{3,2,1,0:T(8,128)S(1)}, f32[3,2,32,256]{3,2,1,0:T(8,128)S(1)}, u32[]{:S(2)}, u32[]{:S(2)}) collective-permute-start(f32[3,2,32,256]{3,2,1,0:T(8,128)S(1)} %get-tuple-element.58), channel_id=1, source_target_pairs={{0,2},{2,0},{4,6},{6,4},{8,10},{10,8},{12,14},{14,12},{16,18},{18,... | collective-permute-start | bytes 589832 | tf_op jit(solution)/shard_map/ppermute | solution.py:451
  55.3 8.5 %collective-permute-start.14 = (f32[3,2,32,256]{3,2,1,0:T(8,128)S(1)}, f32[3,2,32,256]{3,2,1,0:T(8,128)S(1)}, u32[]{:S(2)}, u32[]{:S(2)}) collective-permute-start(f32[3,2,32,256]{3,2,1,0:T(8,128)S(1)} %get-tuple-element.59), channel_id=1, source_target_pairs={{0,4},{2,6},{4,0},{6,2},{8,12},{10,14},{12,8},{14,10},{16,20},{18,... | collective-permute-start | bytes 589832 | tf_op jit(solution)/shard_map/ppermute | solution.py:451
  57.1 9.8 %collective-permute-start.16 = (f32[2,2,32,256]{3,2,1,0:T(8,128)S(1)}, f32[2,2,32,256]{3,2,1,0:T(8,128)S(1)}, u32[]{:S(2)}, u32[]{:S(2)}) collective-permute-start(f32[2,2,32,256]{3,2,1,0:T(8,128)S(1)} %pack_sums.2.refs_5_), channel_id=1, source_target_pairs={{0,16},{2,18},{4,20},{6,22},{8,24},{10,26},{12,28},{14,30},{16,0},... | collective-permute-start | bytes 393224 | tf_op jit(solution)/shard_map/ppermute | solution.py:451
  69.7 7.4 %collective-permute-start.21 = (f32[2,2,32,256]{3,2,1,0:T(8,128)S(1)}, f32[2,2,32,256]{3,2,1,0:T(8,128)S(1)}, u32[]{:S(2)}, u32[]{:S(2)}) collective-permute-start(f32[2,2,32,256]{3,2,1,0:T(8,128)S(1)} %tmat_apply.4.own_ref.refs_3_), channel_id=1, source_target_pairs={{0,8},{2,10},{4,12},{6,14},{8,0},{10,2},{12,4},{14,6},{16,24},{18,... | collective-permute-start | bytes 393224 | tf_op jit(solution)/shard_map/ppermute | solution.py:451
  72.6 5.5 %collective-permute-start.20 = (f32[2,2,32,256]{3,2,1,0:T(8,128)S(1)}, f32[2,2,32,256]{3,2,1,0:T(8,128)S(1)}, u32[]{:S(2)}, u32[]{:S(2)}) collective-permute-start(f32[2,2,32,256]{3,2,1,0:T(8,128)S(1)} %tmat_apply.4.own_ref.refs_3_), channel_id=1, source_target_pairs={{0,4},{2,6},{4,0},{6,2},{8,12},{10,14},{12,8},{14,10},{16,20},{18,... | collective-permute-start | bytes 393224 | tf_op jit(solution)/shard_map/ppermute | solution.py:451
  74.0 5.2 %collective-permute-start.19 = (f32[2,2,32,256]{3,2,1,0:T(8,128)S(1)}, f32[2,2,32,256]{3,2,1,0:T(8,128)S(1)}, u32[]{:S(2)}, u32[]{:S(2)}) collective-permute-start(f32[2,2,32,256]{3,2,1,0:T(8,128)S(1)} %tmat_apply.4.own_ref.refs_3_), channel_id=1, source_target_pairs={{0,2},{2,0},{4,6},{6,4},{8,10},{10,8},{12,14},{14,12},{16,18},{18,... | collective-permute-start | bytes 393224 | tf_op jit(solution)/shard_map/ppermute | solution.py:451
  79.3 8.8 %collective-permute-start.22 = (f32[5,2,32,256]{3,2,1,0:T(8,128)S(1)}, f32[5,2,32,256]{3,2,1,0:T(8,128)S(1)}, u32[]{:S(2)}, u32[]{:S(2)}) collective-permute-start(f32[5,2,32,256]{3,2,1,0:T(8,128)S(1)} %get-tuple-element.62), channel_id=1, source_target_pairs={{0,2},{2,0},{4,6},{6,4},{8,10},{10,8},{12,14},{14,12},{16,18},{18,... | collective-permute-start | bytes 983048 | tf_op jit(solution)/shard_map/ppermute | solution.py:451
  79.6 8.6 %collective-permute-start.23 = (f32[5,2,32,256]{3,2,1,0:T(8,128)S(1)}, f32[5,2,32,256]{3,2,1,0:T(8,128)S(1)}, u32[]{:S(2)}, u32[]{:S(2)}) collective-permute-start(f32[5,2,32,256]{3,2,1,0:T(8,128)S(1)} %get-tuple-element.63), channel_id=1, source_target_pairs={{0,4},{2,6},{4,0},{6,2},{8,12},{10,14},{12,8},{14,10},{16,20},{18,... | collective-permute-start | bytes 983048 | tf_op jit(solution)/shard_map/ppermute | solution.py:451
  80.3 7.8 %collective-permute-start.24 = (f32[2,2,32,256]{3,2,1,0:T(8,128)S(1)}, f32[2,2,32,256]{3,2,1,0:T(8,128)S(1)}, u32[]{:S(2)}, u32[]{:S(2)}) collective-permute-start(f32[2,2,32,256]{3,2,1,0:T(8,128)S(1)} %get-tuple-element.64), channel_id=1, source_target_pairs={{0,16},{2,18},{4,20},{6,22},{8,24},{10,26},{12,28},{14,30},{16,0},... | collective-permute-start | bytes 393224 | tf_op jit(solution)/shard_map/ppermute | solution.py:451
  88.3 13.1 %collective-permute-start.25 = (f32[8,2,32,256]{3,2,1,0:T(8,128)S(1)}, f32[8,2,32,256]{3,2,1,0:T(8,128)S(1)}, u32[]{:S(2)}, u32[]{:S(2)}) collective-permute-start(f32[8,2,32,256]{3,2,1,0:T(8,128)S(1)} %get-tuple-element.66), channel_id=1, source_target_pairs={{0,2},{2,0},{4,6},{6,4},{8,10},{10,8},{12,14},{14,12},{16,18},{18,... | collective-permute-start | bytes 1572872 | tf_op jit(solution)/shard_map/ppermute | solution.py:451
  89.8 12.5 %collective-permute-start.26 = (f32[8,2,32,256]{3,2,1,0:T(8,128)S(1)}, f32[8,2,32,256]{3,2,1,0:T(8,128)S(1)}, u32[]{:S(2)}, u32[]{:S(2)}) collective-permute-start(f32[8,2,32,256]{3,2,1,0:T(8,128)S(1)} %get-tuple-element.67), channel_id=1, source_target_pairs={{0,4},{2,6},{4,0},{6,2},{8,12},{10,14},{12,8},{14,10},{16,20},{18,... | collective-permute-start | bytes 1572872 | tf_op jit(solution)/shard_map/ppermute | solution.py:451
  91.0 7.3 %collective-permute-start.27 = (f32[2,2,32,256]{3,2,1,0:T(8,128)S(1)}, f32[2,2,32,256]{3,2,1,0:T(8,128)S(1)}, u32[]{:S(2)}, u32[]{:S(2)}) collective-permute-start(f32[2,2,32,256]{3,2,1,0:T(8,128)S(1)} %get-tuple-element.68), channel_id=1, source_target_pairs={{0,16},{2,18},{4,20},{6,22},{8,24},{10,26},{12,28},{14,30},{16,0},... | collective-permute-start | bytes 393224 | tf_op jit(solution)/shard_map/ppermute | solution.py:451
  102.3 8.8 %collective-permute-start.28 = (f32[6,2,32,256]{3,2,1,0:T(8,128)S(1)}, f32[6,2,32,256]{3,2,1,0:T(8,128)S(1)}, u32[]{:S(2)}, u32[]{:S(2)}) collective-permute-start(f32[6,2,32,256]{3,2,1,0:T(8,128)S(1)} %get-tuple-element.69), channel_id=1, source_target_pairs={{0,2},{2,0},{4,6},{6,4},{8,10},{10,8},{12,14},{14,12},{16,18},{18,... | collective-permute-start | bytes 1179656 | tf_op jit(solution)/shard_map/ppermute | solution.py:451
  103.3 8.9 %collective-permute-start.29 = (f32[6,2,32,256]{3,2,1,0:T(8,128)S(1)}, f32[6,2,32,256]{3,2,1,0:T(8,128)S(1)}, u32[]{:S(2)}, u32[]{:S(2)}) collective-permute-start(f32[6,2,32,256]{3,2,1,0:T(8,128)S(1)} %get-tuple-element.70), channel_id=1, source_target_pairs={{0,4},{2,6},{4,0},{6,2},{8,12},{10,14},{12,8},{14,10},{16,20},{18,... | collective-permute-start | bytes 1179656 | tf_op jit(solution)/shard_map/ppermute | solution.py:451
  104.8 9.7 %collective-permute-start.32 = (f32[4,2,32,256]{3,2,1,0:T(8,128)S(1)}, f32[4,2,32,256]{3,2,1,0:T(8,128)S(1)}, u32[]{:S(2)}, u32[]{:S(2)}) collective-permute-start(f32[4,2,32,256]{3,2,1,0:T(8,128)S(1)} %get-tuple-element.75), channel_id=1, source_target_pairs={{0,8},{2,10},{4,12},{6,14},{8,0},{10,2},{12,4},{14,6},{16,24},{18,... | collective-permute-start | bytes 786440 | tf_op jit(solution)/shard_map/ppermute | solution.py:451
  112.3 7.5 %collective-permute-start.30 = (f32[3,2,32,256]{3,2,1,0:T(8,128)S(1)}, f32[3,2,32,256]{3,2,1,0:T(8,128)S(1)}, u32[]{:S(2)}, u32[]{:S(2)}) collective-permute-start(f32[3,2,32,256]{3,2,1,0:T(8,128)S(1)} %get-tuple-element.72), channel_id=1, source_target_pairs={{0,2},{2,0},{4,6},{6,4},{8,10},{10,8},{12,14},{14,12},{16,18},{18,... | collective-permute-start | bytes 589832 | tf_op jit(solution)/shard_map/ppermute | solution.py:451
  113.0 6.8 %collective-permute-start.31 = (f32[3,2,32,256]{3,2,1,0:T(8,128)S(1)}, f32[3,2,32,256]{3,2,1,0:T(8,128)S(1)}, u32[]{:S(2)}, u32[]{:S(2)}) collective-permute-start(f32[3,2,32,256]{3,2,1,0:T(8,128)S(1)} %get-tuple-element.73), channel_id=1, source_target_pairs={{0,4},{2,6},{4,0},{6,2},{8,12},{10,14},{12,8},{14,10},{16,20},{18,... | collective-permute-start | bytes 589832 | tf_op jit(solution)/shard_map/ppermute | solution.py:451
  114.5 8.4 %collective-permute-start.33 = (f32[2,2,32,256]{3,2,1,0:T(8,128)S(1)}, f32[2,2,32,256]{3,2,1,0:T(8,128)S(1)}, u32[]{:S(2)}, u32[]{:S(2)}) collective-permute-start(f32[2,2,32,256]{3,2,1,0:T(8,128)S(1)} %pack_sums.3.refs_5_), channel_id=1, source_target_pairs={{0,16},{2,18},{4,20},{6,22},{8,24},{10,26},{12,28},{14,30},{16,0},... | collective-permute-start | bytes 393224 | tf_op jit(solution)/shard_map/ppermute | solution.py:451
  (7 other events, 11.6 us)
where the time goes:
time: 126 us
  Pallas kernels  59.8 us (47%)
  starting transfers between devices  43.8 us (35%)
  waiting for transfers between devices  16.9 us (13%)
  local copies, waits for them, and re-layouts  3.85 us (3%)
  between operations  1.67 us (1%)
    ppermute x30, starting transfers between devices, across(): lax.ppermute(value, 'owner', [(source, source ^ bit) for source in range(...  42.9 us
    pallas_call x8, Pallas kernels, forward(): pl.pallas_call(functools.partial(forward_kernel, groups, copies, len(fiel...  27.7 us
    pallas_call x6, Pallas kernels, backward(): pl.pallas_call(functools.partial(backward_kernel, first, groups, base), o...  25.7 us
    ppermute x30, waiting for transfers between devices, across(): lax.ppermute(value, 'owner', [(source, source ^ bit) for source in range(...  13.9 us
    unnamed x8, local copies, waits for them, and re-layouts  3.85 us
    pallas_call x3, Pallas kernels, apply_tmat(): pl.pallas_call(functools.partial(tmat_kernel, halves), out_shape=[half_sh...  3.3 us
    ppermute x5, waiting for transfers between devices, from_other(): return lax.ppermute(value, 'pair', [(0, 1), (1, 0)])  3.05 us
  transfers between devices with their start and end apart: 35, of which 13 were waited for; matrix products, arithmetic and copies ran while one was open for 0% of the time, Pallas kernels for 44%

commit v1 on v0

--- a/solution.py
+++ b/solution.py
@@ -67,6 +67,7 @@
     for group in range(GROUPS):
         index_ref[counts + group] = 0
     index_ref[counts + GROUPS] = side_ref[0]
+    index_ref[counts + GROUPS + 1] = my_layer
 
     def step(slot, carry):
         row = rows_of_ref[partners_ref[me * slots + slot]]
@@ -91,7 +92,7 @@
     slots = block_rows.shape[0]
     return pl.pallas_call(
         functools.partial(index_kernel, layers, particles),
-        out_shape=jax.ShapeDtypeStruct((3 * GROUPS * slots + GROUPS + 1,), jnp.int32),
+        out_shape=jax.ShapeDtypeStruct((3 * GROUPS * slots + GROUPS + 2,), jnp.int32),
         in_specs=[SMEM] * 6,
         out_specs=SMEM,
         compiler_params=pltpu.CompilerParams(vmem_limit_bytes=ALONE_LIMIT),
@@ -177,6 +178,12 @@
         compiler_params=params(3 * size_of(mine, theirs), size_of(parts)),
         name="tmat_apply",
     )(side, mine, theirs, parts)
+
+
+def row_from(row, my_layer):
+    if isinstance(row, tuple):
+        return lax.bitwise_xor(my_layer, row[0]) * row[2] + row[1]
+    return row
 
 
 def chosen_slots(index_ref, groups, slots):
@@ -336,8 +343,9 @@
             fetch(early, early).start()
 
     acc_ref[...] = refs[count + 1][...] if begun else jnp.zeros_like(acc_ref)
+    my_layer = index_ref[3 * GROUPS * parts_ref.shape[0] + GROUPS + 1]
     for number, row, place in copies:
-        every_ref[place] = field_refs[number][row]
+        every_ref[place] = field_refs[number][row_from(row, my_layer)]
 
     def body(turn, carry):
         here = lax.rem(turn, BUFFERS)
@@ -391,26 +399,27 @@
     )(index, *fields, parts, *given, *after)
 
 
-def pack_kernel(plans, count, *refs):
+def pack_kernel(plans, count, layer_ref, *refs):
     in_refs, out_refs = refs[:count], refs[-len(plans) :]
+    my_layer = layer_ref[0]
     for out_ref, plan in zip(out_refs, plans):
         for row, terms in enumerate(plan):
-            value = in_refs[terms[0][0]][terms[0][1]]
+            value = in_refs[terms[0][0]][row_from(terms[0][1], my_layer)]
             for number, source in terms[1:]:
-                value = value + in_refs[number][source]
+                value = value + in_refs[number][row_from(source, my_layer)]
             out_ref[row] = value
 
 
-def pack(name, inputs, plans, after=()):
+def pack(name, inputs, plans, after=(), *, my_layer):
     shapes = [jax.ShapeDtypeStruct((len(plan),) + inputs[0].shape[1:], F32) for plan in plans]
     return pl.pallas_call(
         functools.partial(pack_kernel, plans, len(inputs)),
         out_shape=shapes,
-        in_specs=[VMEM] * len(inputs) + [ANY] * len(after),
+        in_specs=[SMEM] + [VMEM] * len(inputs) + [ANY] * len(after),
         out_specs=[VMEM] * len(plans),
         compiler_params=params(size_of(*inputs), size_of(*shapes)),
         name=name,
-    )(*inputs, *after)
+    )(my_layer, *inputs, *after)
 
 
 def total_kernel(counts, side_ref, incident_ref, *refs):
@@ -451,7 +460,7 @@
     return lax.ppermute(value, "owner", [(source, source ^ bit) for source in range(count)])
 
 
-def scatter_step(incident, scattered, blocks, parts, index, side, layers):
+def scatter_step(incident, scattered, blocks, parts, index, side, my_layer, layers):
     particles = incident.shape[0]
     every = range(particles)
     by_x = range((particles + 1) // 2)
@@ -462,6 +471,7 @@
     total_rows = COLUMNS * particles * layers
     first_n, first_d = at(1, 0, 0), at(3, 0, 0)
     first = parts is None
+    joined = functools.partial(pack, my_layer=my_layer)
 
     def row_of(particle, layer):
         return particle * layers + layer
@@ -469,8 +479,8 @@
     other = from_other(scattered)
     x1 = across(scattered, 1)
     y1 = across(scattered, 2)
-    reached = [across(scattered, COLUMNS)]
-    where = {1: (0, 0), 2: (1, 0), 3: (2, 0)}
+    columns = [[column + COLUMNS * layer for layer in range(layers)] for column in range(COLUMNS)]
+    reached = lax.all_gather(scattered, "owner", axis_index_groups=columns, axis=0, tiled=True)
     fetched = (scattered, other, blocks)
     products_d, *made = backward(
         first, (2, 4), first_d, total_rows - first_d, index, *fetched, parts
@@ -478,29 +488,19 @@
     if first:
         parts = made[0]
 
-    inputs = [products_d, x1, y1, scattered]
+    inputs = [products_d, x1, y1]
     x_plan = [[(0, row_of(particle, layer))] for particle in by_x for layer in range(layers)]
     y_plan = [[(0, row_of(particle, layer))] for particle in by_y for layer in range(layers)]
     x_head, y_head = len(x_plan), len(y_plan)
     x_plan += [[(2, particle)] for particle in by_y]
     y_plan += [[(1, particle)] for particle in by_x]
-    x2, y2, copied = pack(
-        "pack_second",
-        inputs,
-        [x_plan, y_plan, [[(3, particle)] for particle in every]],
-        reached,
-    )
+    x2, y2 = joined("pack_second", inputs, [x_plan, y_plan])
     x2, y2 = across(x2, 1), across(y2, 2)
-    reached.append(across(copied, 2 * COLUMNS))
     products_n, *made = backward(first, (1, 3), first_n, first_d - first_n, index, *fetched, parts)
     if first:
         parts = made[0]
 
-    def z_row(particle, layer):
-        number, start = where[layer]
-        return number, start + particle
-
-    inputs = [products_n, x2, y2, scattered, reached[0]]
+    inputs = [products_n, x2, y2, scattered]
     x_plan, y_plan = [], []
     for particle in every:
         for layer in range(layers):
@@ -512,18 +512,10 @@
                 x_terms.append((2, row_of(particle - len(by_x), layer)))
             x_plan.append(x_terms)
             y_plan.append(y_terms)
-    z_plans = [[[(number, particle)] for particle in every] for number in (3, 4)]
-    x3, y3, copied, known = pack("pack_third", inputs, [x_plan, y_plan] + z_plans, reached[1:])
+    x3, y3, copied = joined(
+        "pack_third", inputs, [x_plan, y_plan, [[(3, particle)] for particle in every]]
+    )
     x3, y3 = across(x3, 1), across(y3, 2)
-    reached.append(across(known, 2 * COLUMNS))
-    for bit in powers[2:]:
-        plan = [[(0, particle)] for particle in every]
-        for layer in range(1, bit):
-            plan += [[(1 + where[layer][0], where[layer][1] + particle)] for particle in every]
-        (known,) = pack("pack_layers", [scattered] + reached, [plan])
-        for layer in range(bit):
-            where[bit + layer] = (len(reached), layer * particles)
-        reached.append(across(known, bit * COLUMNS))
     products_o, *made = backward(first, (0,), 0, first_n, index, copied, other, blocks, parts)
     if first:
         parts = made[0]
@@ -550,13 +542,9 @@
         chosen = range(bit, layers, 2 * bit)
         return [summed(layer, particle, arrived) for layer in chosen for particle in every]
 
-    inputs = [products_o, x3, y3] + reached
-    tails = []
-    for particle in every:
-        for layer in rest:
-            step, row = z_row(particle, layer)
-            tails.append([(3 + step, row)])
-    x4, y4, sums, mark = pack(
+    inputs = [products_o, x3, y3, reached]
+    tails = [[(3, (layer, particle, particles))] for particle in every for layer in rest]
+    x4, y4, sums, mark = joined(
         "pack_fourth",
         inputs,
         [tails, tails, half_sums(1, 0), [[(1, 0)]]],
@@ -567,14 +555,13 @@
     copies = []
     for particle in every:
         for layer in rest:
-            step, row = z_row(particle, layer)
-            copies.append((step, row, at(0, particle, layer)))
-    near = forward((0,), index, reached, tuple(copies), parts, *sizes, near, False, [mark])
+            copies.append((0, (layer, particle, particles), at(0, particle, layer)))
+    near = forward((0,), index, [reached], tuple(copies), parts, *sizes, near, False, [mark])
 
     def tail(particle, layer):
         return particle * len(rest) + layer - 1
 
-    x5, y5, mark = pack(
+    x5, y5, mark = joined(
         "pack_fifth",
         [x4, y4],
         [
@@ -587,7 +574,7 @@
     x5, y5 = across(x5, 1), across(y5, 2)
     for bit in powers[1:]:
         inputs = [products_o, x3, y3] + arrived
-        (sums,) = pack("pack_sums", inputs, [half_sums(bit, len(arrived))], [mark])
+        (sums,) = joined("pack_sums", inputs, [half_sums(bit, len(arrived))], [mark])
         arrived.append(across(sums, bit * COLUMNS))
     copies = []
     for particle in every:
@@ -609,6 +596,7 @@
     layers = lax.axis_size("owner") // COLUMNS
     my_owner = lax.axis_index("owner").astype(jnp.int32)[None]
     side = lax.axis_index("pair").astype(jnp.int32)[None]
+    my_layer = my_owner // COLUMNS
     theirs = from_other(incident)
     index = slot_index(
         my_owner, side, partners, owner_of, block_rows, live, layers, incident.shape[0]
@@ -617,7 +605,7 @@
     (scattered,) = apply_tmat(True, False, side, incident, theirs, tmat_parts)
     parts = None
     for turn in range(ITERS):
-        mine, parts = scatter_step(incident, scattered, blocks, parts, index, side, layers)
+        mine, parts = scatter_step(incident, scattered, blocks, parts, index, side, my_layer, layers)
         theirs = from_other(mine)
         last = turn == ITERS - 1
         *exciting, scattered = apply_tmat(False, last, side, mine, theirs, tmat_parts)

time: 126 us -> 146 us (1.16); the launches traced: 126 us -> 144 us
  blocking collectives: 0 us -> 30.6 us
  starting transfers between devices: 43.8 us -> 16.3 us
  Pallas kernels: 59.8 us -> 73.6 us
    all_gather x0 -> x2, blocking collectives: none -> 30.6 us  [scatter_step(): lax.all_gather(scattered, 'owner', axis_index_groups=columns, axis=0, til...]
    ppermute x30 -> x24, starting transfers between devices: 42.9 us -> 15.4 us  [across(): lax.ppermute(value, 'owner', [(source, source ^ bit) for source in range(...]
    pallas_call x6, Pallas kernels: 25.7 us -> 33.1 us  [backward(): pl.pallas_call(functools.partial(backward_kernel, first, groups, base), o...]
    pallas_call x8, Pallas kernels: 27.7 us -> 33.9 us  [forward(): pl.pallas_call(functools.partial(forward_kernel, groups, copies, len(fiel...]
    ppermute x30 -> x24, waiting for transfers between devices: 13.9 us -> 13.9 us  [across(): lax.ppermute(value, 'owner', [(source, source ^ bit) for source in range(...]
  transfers between devices with their start and end apart: 35 -> 29, of which waited for: 13 -> 8; matrix products, arithmetic and copies ran while one was open for 0% -> 0% of each run, Pallas kernels for 44% -> 48%
where the time goes in v1:
time: 146 us; the launch traced here: 144 us
  Pallas kernels  73.6 us (50%)
  blocking collectives  30.6 us (21%)
  waiting for transfers between devices  18.1 us (12%)
  starting transfers between devices  16.3 us (11%)
  local copies, waits for them, and re-layouts  3.85 us (3%)
  between operations  1.67 us (1%)
    pallas_call x8, Pallas kernels, forward(): pl.pallas_call(functools.partial(forward_kernel, groups, copies, len(fiel...  33.9 us
    pallas_call x6, Pallas kernels, backward(): pl.pallas_call(functools.partial(backward_kernel, first, groups, base), o...  33.1 us
    all_gather x2, blocking collectives, scatter_step(): lax.all_gather(scattered, 'owner', axis_index_groups=columns, axis=0, til...  30.6 us
    ppermute x24, starting transfers between devices, across(): lax.ppermute(value, 'owner', [(source, source ^ bit) for source in range(...  15.4 us
    ppermute x24, waiting for transfers between devices, across(): lax.ppermute(value, 'owner', [(source, source ^ bit) for source in range(...  13.9 us
    ppermute x5, waiting for transfers between devices, from_other(): return lax.ppermute(value, 'pair', [(0, 1), (1, 0)])  4.23 us
    unnamed x8, local copies, waits for them, and re-layouts  3.85 us
    pallas_call x3, Pallas kernels, apply_tmat(): pl.pallas_call(functools.partial(tmat_kernel, halves), out_shape=[half_sh...  3.31 us
  transfers between devices with their start and end apart: 29, of which 8 were waited for; matrix products, arithmetic and copies ran while one was open for 0% of the time, Pallas kernels for 48%

profile of v1, /device:TPU:0, one launch (start us, length us, event | category | flops | bytes accessed | tf_op | source)
XLA Modules:
  0.0 144.2 jit_solution(5590386417251481635)
XLA Ops:
  1.8 1.9 %slot_index.1.after_ref.index_ref = s32[322]{0:T(512)} custom-call(s32[1]{0:T(128)} %bitcast.1.owner_ref, s32[1]{0:T(128)} %bitcast.side_ref, s32[336]{0:T(512)} %partners_ref.1, s32[32]{0:T(128)} %rows_of_ref.1, s32[21]{0:T(128)} %holders_ref.1, s32[1]{0:T(128)S(6)} %copy.13.live_ref), custom_call_target="tpu_custom_call" | custom-call | tf_op jit(solution)/shard_map/slot_index/pallas_call | solution.py:93
  3.7 1.6 %copy-done = f32[2,2,256,512]{3,2,1,0:T(8,128)S(1)} copy-done((f32[2,2,256,512]{3,2,1,0:T(8,128)S(1)}, f32[2,2,256,512]{3,2,1,0:T(8,128)}, u32[]{:S(2)}) %copy-start) | copy-done | bytes 2097176
  8.6 2.7 %collective-permute-start.2 = (f32[2,2,32,256]{3,2,1,0:T(8,128)S(1)}, f32[2,2,32,256]{3,2,1,0:T(8,128)S(1)}, u32[]{:S(2)}, u32[]{:S(2)}) collective-permute-start(f32[2,2,32,256]{3,2,1,0:T(8,128)S(1)} %tmat_apply.3.own_ref.refs_3_), channel_id=1, source_target_pairs={{0,2},{2,0},{4,6},{6,4},{8,10},{10,8},{12,14},{14,12},{16,18},{18,... | collective-permute-start | bytes 393224 | tf_op jit(solution)/shard_map/ppermute | solution.py:460
  11.3 1.2 collective-permute-start.3
  13.3 5.3 %backward_group2.2 = (f32[8,2,32,256]{3,2,1,0:T(8,128)S(1)}, bf16[21,2,2,512,256]{4,3,2,1,0:T(8,128)(2,1)}) custom-call(s32[322]{0:T(512)S(1)} %copy-done.2, f32[2,2,32,256]{3,2,1,0:T(8,128)S(1)} %tmat_apply.3.own_ref.refs_3_, f32[2,2,32,256]{3,2,1,0:T(8,128)S(1)} %collective-permute-done.1.other_ref, f32[21,2,512,256]{3,2,1,0:T(8,128)} %blocks_ref.5), custom_call_target="tpu_custom_call" | custom-call | flops 4194304 | bytes 131072 | tf_op jit(solution)/shard_map/backward_group2/pallas_call | solution.py:307
  18.8 10.2 %backward_group1.2 = (f32[16,2,32,256]{3,2,1,0:T(8,128)S(1)}, bf16[21,2,2,512,256]{4,3,2,1,0:T(8,128)(2,1)}) custom-call(s32[322]{0:T(512)S(1)} %copy-done.2, f32[2,2,32,256]{3,2,1,0:T(8,128)S(1)} %tmat_apply.3.own_ref.refs_3_, f32[2,2,32,256]{3,2,1,0:T(8,128)S(1)} %collective-permute-done.1.other_ref, ...), custom_call_target="tpu_custom_call", output_to_operand_aliasing={{1}: (4, {})} | custom-call | flops 4194304 | bytes 131072 | tf_op jit(solution)/shard_map/backward_group1/pallas_call | solution.py:307
  30.1 15.9 %all_gather.6.refs_3_.refs_0_ = f32[8,2,32,256]{3,2,1,0:T(8,128)S(1)} all-gather(f32[2,2,32,256]{3,2,1,0:T(8,128)S(1)} %tmat_apply.3.own_ref.refs_3_), channel_id=1, replica_groups={{0,8,16,24},{2,10,18,26},{4,12,20,28},{6,14,22,30},{1,9,17,25},{3,11,19..., dimensions={0}, use_global_device_ids=true | all-gather | bytes 655360 | tf_op jit(solution)/shard_map/all_gather | solution.py:483
  45.9 4.6 %backward_group0.2 = (f32[8,2,32,256]{3,2,1,0:T(8,128)S(1)}, bf16[21,2,2,512,256]{4,3,2,1,0:T(8,128)(2,1)}) custom-call(s32[322]{0:T(512)S(1)} %copy-done.2, f32[2,2,32,256]{3,2,1,0:T(8,128)S(1)} %get-tuple-element.43.own_ref, f32[2,2,32,256]{3,2,1,0:T(8,128)S(1)} %collective-permute-done.1.other_ref, ...), custom_call_target="tpu_custom_call", output_to_operand_aliasing={{1}: (4, {})} | custom-call | flops 4194304 | bytes 131072 | tf_op jit(solution)/shard_map/backward_group0/pallas_call | solution.py:307
  50.5 4.5 %forward_group1.2.refs_4_.refs_2_ = f32[2,512,128]{2,1,0:T(8,128)S(1)} custom-call(s32[322]{0:T(512)S(1)} %copy-done.2, f32[2,2,32,256]{3,2,1,0:T(8,128)S(1)} %collective-permute-done.2.refs_1_.refs_0_, f32[2,2,32,256]{3,2,1,0:T(8,128)S(1)} %collective-permute-done.3.refs_2_.refs_1_, f32[5,2,32,256]{3,2,1,0:T(8,128)S(1)} %collective-permute-done.4.refs_1_.refs_2_, ...), custom_call_target="tpu_custom_call" | custom-call | flops 4194304 | bytes 524288 | tf_op jit(solution)/shard_map/forward_group1/pallas_call | solution.py:386
  55.6 3.6 %forward_group0.2.refs_2_.refs_3_ = f32[2,512,128]{2,1,0:T(8,128)S(1)} custom-call(s32[322]{0:T(512)S(1)} %copy-done.2, f32[8,2,32,256]{3,2,1,0:T(8,128)S(1)} %all_gather.6.refs_3_.refs_0_, bf16[21,2,2,512,256]{4,3,2,1,0:T(8,128)(2,1)} %get-tuple-element.48.refs_4_.refs_1_.refs_2_.blocks_ref, f32[2,512,128]{2,1,0:T(8,128)S(1)} %forward_group1.2.refs_4_.refs_2_, ...), custom_call_target="tpu_custom_call" | custom-call | flops 4194304 | bytes 524288 | tf_op jit(solution)/shard_map/forward_group0/pallas_call | solution.py:386
  59.2 5.3 %collective-permute-done.8.refs_0_ = f32[6,2,32,256]{3,2,1,0:T(8,128)S(1)} collective-permute-done((f32[6,2,32,256]{3,2,1,0:T(8,128)S(1)}, f32[6,2,32,256]{3,2,1,0:T(8,128)S(1)}, u32[]{:S(2)}, u32[]{:S(2)}) %collective-permute-start.8) | collective-permute-done | bytes 393248 | tf_op jit(solution)/shard_map/ppermute | solution.py:460
  64.5 2.3 %collective-permute-start.10 = (f32[3,2,32,256]{3,2,1,0:T(8,128)S(1)}, f32[3,2,32,256]{3,2,1,0:T(8,128)S(1)}, u32[]{:S(2)}, u32[]{:S(2)}) collective-permute-start(f32[3,2,32,256]{3,2,1,0:T(8,128)S(1)} %get-tuple-element.52), channel_id=1, source_target_pairs={{0,2},{2,0},{4,6},{6,4},{8,10},{10,8},{12,14},{14,12},{16,18},{18,... | collective-permute-start | bytes 589832 | tf_op jit(solution)/shard_map/ppermute | solution.py:460
  66.9 1.0 collective-permute-start.13
  67.8 5.4 %forward_group3.2.refs_3_ = f32[2,512,128]{2,1,0:T(8,128)S(1)} custom-call(s32[322]{0:T(512)S(1)} %copy-done.2, f32[6,2,32,256]{3,2,1,0:T(8,128)S(1)} %collective-permute-done.8.refs_0_, f32[6,2,32,256]{3,2,1,0:T(8,128)S(1)} %collective-permute-done.9.refs_1_, bf16[21,2,2,512,256]{4,3,2,1,0:T(8,128)(2,1)} %get-tuple-element.48.refs_4_.refs_1_.refs_2_.blocks_ref, ...), custom_call_target="tpu_custom_call" | custom-call | flops 4194304 | bytes 524288 | tf_op jit(solution)/shard_map/forward_group3/pallas_call | solution.py:386
  73.2 3.5 %forward_group4.2.refs_0_ = f32[2,2,32,512]{3,2,1,0:T(8,128)S(1)} custom-call(s32[322]{0:T(512)S(1)} %copy-done.2, f32[3,2,32,256]{3,2,1,0:T(8,128)S(1)} %collective-permute-done.10.refs_0_, f32[3,2,32,256]{3,2,1,0:T(8,128)S(1)} %collective-permute-done.11.refs_1_, bf16[21,2,2,512,256]{4,3,2,1,0:T(8,128)(2,1)} %get-tuple-element.48.refs_4_.refs_1_.refs_2_.blocks_ref, ...), custom_call_target="tpu_custom_call" | custom-call | flops 4194304 | bytes 262144 | tf_op jit(solution)/shard_map/forward_group4/pallas_call | solution.py:386
  76.9 1.5 %collective-permute-done.14.theirs_ref = f32[2,2,32,512]{3,2,1,0:T(8,128)S(1)} collective-permute-done((f32[2,2,32,512]{3,2,1,0:T(8,128)S(1)}, f32[2,2,32,512]{3,2,1,0:T(8,128)S(1)}, u32[]{:S(2)}, u32[]{:S(2)}) %collective-permute-start.14) | collective-permute-done | bytes 262176 | tf_op jit(solution)/shard_map/ppermute | solution.py:455
  79.5 1.2 collective-permute-done.15.other_ref
  80.7 3.7 %backward_group2.3.refs_0_ = f32[8,2,32,256]{3,2,1,0:T(8,128)S(1)} custom-call(s32[322]{0:T(512)S(1)} %copy-done.2, f32[2,2,32,256]{3,2,1,0:T(8,128)S(1)} %tmat_apply.4.own_ref.refs_3_, f32[2,2,32,256]{3,2,1,0:T(8,128)S(1)} %collective-permute-done.15.other_ref, bf16[21,2,2,512,256]{4,3,2,1,0:T(8,128)(2,1)} %get-tuple-element.48.refs_4_.refs_1_.refs_2_.blocks_ref), custom_call_target="tpu_custom_call" | custom-call | flops 4194304 | bytes 131072 | tf_op jit(solution)/shard_map/backward_group2/pallas_call | solution.py:307
  85.3 1.8 %collective-permute-start.18 = (f32[5,2,32,256]{3,2,1,0:T(8,128)S(1)}, f32[5,2,32,256]{3,2,1,0:T(8,128)S(1)}, u32[]{:S(2)}, u32[]{:S(2)}) collective-permute-start(f32[5,2,32,256]{3,2,1,0:T(8,128)S(1)} %get-tuple-element.56), channel_id=1, source_target_pairs={{0,2},{2,0},{4,6},{6,4},{8,10},{10,8},{12,14},{14,12},{16,18},{18,... | collective-permute-start | bytes 983048 | tf_op jit(solution)/shard_map/ppermute | solution.py:460
  87.4 6.2 %backward_group1.3.refs_0_ = f32[16,2,32,256]{3,2,1,0:T(8,128)S(1)} custom-call(s32[322]{0:T(512)S(1)} %copy-done.2, f32[2,2,32,256]{3,2,1,0:T(8,128)S(1)} %tmat_apply.4.own_ref.refs_3_, f32[2,2,32,256]{3,2,1,0:T(8,128)S(1)} %collective-permute-done.15.other_ref, bf16[21,2,2,512,256]{4,3,2,1,0:T(8,128)(2,1)} %get-tuple-element.48.refs_4_.refs_1_.refs_2_.blocks_ref), custom_call_target="tpu_custom_call" | custom-call | flops 4194304 | bytes 131072 | tf_op jit(solution)/shard_map/backward_group1/pallas_call | solution.py:307
  93.6 0.9 collective-permute-done.18.refs_1_.refs_2_
  94.6 1.1 collective-permute-done.19.refs_2_.refs_3_
  97.0 14.7 %all_gather.7.refs_3_.refs_0_ = f32[8,2,32,256]{3,2,1,0:T(8,128)S(1)} all-gather(f32[2,2,32,256]{3,2,1,0:T(8,128)S(1)} %tmat_apply.4.own_ref.refs_3_), channel_id=1, replica_groups={{0,8,16,24},{2,10,18,26},{4,12,20,28},{6,14,22,30},{1,9,17,25},{3,11,19..., dimensions={0}, use_global_device_ids=true | all-gather | bytes 655360 | tf_op jit(solution)/shard_map/all_gather | solution.py:483
  111.7 3.1 %backward_group0.3.refs_5_.refs_0_.refs_1_ = f32[8,2,32,256]{3,2,1,0:T(8,128)S(1)} custom-call(s32[322]{0:T(512)S(1)} %copy-done.2, f32[2,2,32,256]{3,2,1,0:T(8,128)S(1)} %get-tuple-element.58.own_ref, f32[2,2,32,256]{3,2,1,0:T(8,128)S(1)} %collective-permute-done.15.other_ref, bf16[21,2,2,512,256]{4,3,2,1,0:T(8,128)(2,1)} %get-tuple-element.48.refs_4_.refs_1_.refs_2_.blocks_ref), custom_call_target="tpu_custom_call" | custom-call | flops 4194304 | bytes 131072 | tf_op jit(solution)/shard_map/backward_group0/pallas_call | solution.py:307
  114.8 4.5 %forward_group1.3.refs_4_.refs_2_ = f32[2,512,128]{2,1,0:T(8,128)S(1)} custom-call(s32[322]{0:T(512)S(1)} %copy-done.2, f32[2,2,32,256]{3,2,1,0:T(8,128)S(1)} %collective-permute-done.16.refs_1_.refs_0_, f32[2,2,32,256]{3,2,1,0:T(8,128)S(1)} %collective-permute-done.17.refs_2_.refs_1_, f32[5,2,32,256]{3,2,1,0:T(8,128)S(1)} %collective-permute-done.18.refs_1_.refs_2_, ...), custom_call_target="tpu_custom_call" | custom-call | flops 4194304 | bytes 524288 | tf_op jit(solution)/shard_map/forward_group1/pallas_call | solution.py:386
  120.2 3.6 %forward_group0.3.refs_2_.refs_3_ = f32[2,512,128]{2,1,0:T(8,128)S(1)} custom-call(s32[322]{0:T(512)S(1)} %copy-done.2, f32[8,2,32,256]{3,2,1,0:T(8,128)S(1)} %all_gather.7.refs_3_.refs_0_, bf16[21,2,2,512,256]{4,3,2,1,0:T(8,128)(2,1)} %get-tuple-element.48.refs_4_.refs_1_.refs_2_.blocks_ref, f32[2,512,128]{2,1,0:T(8,128)S(1)} %forward_group1.3.refs_4_.refs_2_, ...), custom_call_target="tpu_custom_call" | custom-call | flops 4194304 | bytes 524288 | tf_op jit(solution)/shard_map/forward_group0/pallas_call | solution.py:386
  123.8 5.6 %collective-permute-done.22.refs_0_ = f32[6,2,32,256]{3,2,1,0:T(8,128)S(1)} collective-permute-done((f32[6,2,32,256]{3,2,1,0:T(8,128)S(1)}, f32[6,2,32,256]{3,2,1,0:T(8,128)S(1)}, u32[]{:S(2)}, u32[]{:S(2)}) %collective-permute-start.22) | collective-permute-done | bytes 393248 | tf_op jit(solution)/shard_map/ppermute | solution.py:460
  129.4 2.1 %collective-permute-start.24 = (f32[3,2,32,256]{3,2,1,0:T(8,128)S(1)}, f32[3,2,32,256]{3,2,1,0:T(8,128)S(1)}, u32[]{:S(2)}, u32[]{:S(2)}) collective-permute-start(f32[3,2,32,256]{3,2,1,0:T(8,128)S(1)} %get-tuple-element.64), channel_id=1, source_target_pairs={{0,2},{2,0},{4,6},{6,4},{8,10},{10,8},{12,14},{14,12},{16,18},{18,... | collective-permute-start | bytes 589832 | tf_op jit(solution)/shard_map/ppermute | solution.py:460
  132.0 5.4 %forward_group3.3.refs_3_ = f32[2,512,128]{2,1,0:T(8,128)S(1)} custom-call(s32[322]{0:T(512)S(1)} %copy-done.2, f32[6,2,32,256]{3,2,1,0:T(8,128)S(1)} %collective-permute-done.22.refs_0_, f32[6,2,32,256]{3,2,1,0:T(8,128)S(1)} %collective-permute-done.23.refs_1_, bf16[21,2,2,512,256]{4,3,2,1,0:T(8,128)(2,1)} %get-tuple-element.48.refs_4_.refs_1_.refs_2_.blocks_ref, ...), custom_call_target="tpu_custom_call" | custom-call | flops 4194304 | bytes 524288 | tf_op jit(solution)/shard_map/forward_group3/pallas_call | solution.py:386
  137.4 3.5 %forward_group4.3.refs_0_ = f32[2,2,32,512]{3,2,1,0:T(8,128)S(1)} custom-call(s32[322]{0:T(512)S(1)} %copy-done.2, f32[3,2,32,256]{3,2,1,0:T(8,128)S(1)} %collective-permute-done.24.refs_0_, f32[3,2,32,256]{3,2,1,0:T(8,128)S(1)} %collective-permute-done.25.refs_1_, bf16[21,2,2,512,256]{4,3,2,1,0:T(8,128)(2,1)} %get-tuple-element.48.refs_4_.refs_1_.refs_2_.blocks_ref, ...), custom_call_target="tpu_custom_call" | custom-call | flops 4194304 | bytes 262144 | tf_op jit(solution)/shard_map/forward_group4/pallas_call | solution.py:386
  141.1 1.5 %collective-permute-done.28.theirs_ref = f32[2,2,32,512]{3,2,1,0:T(8,128)S(1)} collective-permute-done((f32[2,2,32,512]{3,2,1,0:T(8,128)S(1)}, f32[2,2,32,512]{3,2,1,0:T(8,128)S(1)}, u32[]{:S(2)}, u32[]{:S(2)}) %collective-permute-start.28) | collective-permute-done | bytes 262176 | tf_op jit(solution)/shard_map/ppermute | solution.py:455
  142.6 1.5 %tmat_apply.5 = (f32[2,2,32,256]{3,2,1,0:T(8,128)}, f32[2,2,32,256]{3,2,1,0:T(8,128)}) custom-call(s32[1]{0:T(128)} %bitcast.side_ref, f32[2,2,32,512]{3,2,1,0:T(8,128)S(1)} %total.3.mine_ref, f32[2,2,32,512]{3,2,1,0:T(8,128)S(1)} %collective-permute-done.28.theirs_ref, bf16[2,256,2048]{2,1,0:T(8,128)(2,1)S(1)} %get-tuple-element.37.parts_ref), custom_call_target="tpu_custom_call" | custom-call | tf_op jit(solution)/shard_map/tmat_apply/pallas_call | solution.py:172
  (67 shorter events, 11.6 us)
Async XLA Ops:
  0.6 6.9 %collective-permute-start = (f32[2,2,32,256]{3,2,1,0:T(8,128)}, f32[2,2,32,256]{3,2,1,0:T(8,128)S(1)}, u32[]{:S(2)}, u32[]{:S(2)}) collective-permute-start(f32[2,2,32,256]{3,2,1,0:T(8,128)} %incident_ref.1), channel_id=1, source_target_pairs={{0,1},{1,0},{2,3},{3,2},{4,5},{5,4},{6,7},{7,6},{8,9},{9,8},{10,11... | collective-permute-start | bytes 393224 | tf_op jit(solution)/shard_map/ppermute | solution.py:455
  3.7 1.6 %copy-start = (f32[2,2,256,512]{3,2,1,0:T(8,128)S(1)}, f32[2,2,256,512]{3,2,1,0:T(8,128)}, u32[]{:S(2)}) copy-start(f32[2,2,256,512]{3,2,1,0:T(8,128)} %tmat_ref.1) | copy-start | bytes 6291460
  6.0 0.9 copy-start.3
  8.5 4.1 %collective-permute-start.1 = (f32[2,2,32,256]{3,2,1,0:T(8,128)S(1)}, f32[2,2,32,256]{3,2,1,0:T(8,128)S(1)}, u32[]{:S(2)}, u32[]{:S(2)}) collective-permute-start(f32[2,2,32,256]{3,2,1,0:T(8,128)S(1)} %tmat_apply.3.own_ref.refs_3_), channel_id=1, source_target_pairs={{0,1},{1,0},{2,3},{3,2},{4,5},{5,4},{6,7},{7,6},{8,9},{9,8},{10,11... | collective-permute-start | bytes 393224 | tf_op jit(solution)/shard_map/ppermute | solution.py:455
  8.6 10.0 %collective-permute-start.2 = (f32[2,2,32,256]{3,2,1,0:T(8,128)S(1)}, f32[2,2,32,256]{3,2,1,0:T(8,128)S(1)}, u32[]{:S(2)}, u32[]{:S(2)}) collective-permute-start(f32[2,2,32,256]{3,2,1,0:T(8,128)S(1)} %tmat_apply.3.own_ref.refs_3_), channel_id=1, source_target_pairs={{0,2},{2,0},{4,6},{6,4},{8,10},{10,8},{12,14},{14,12},{16,18},{18,... | collective-permute-start | bytes 393224 | tf_op jit(solution)/shard_map/ppermute | solution.py:460
  11.3 7.3 %collective-permute-start.3 = (f32[2,2,32,256]{3,2,1,0:T(8,128)S(1)}, f32[2,2,32,256]{3,2,1,0:T(8,128)S(1)}, u32[]{:S(2)}, u32[]{:S(2)}) collective-permute-start(f32[2,2,32,256]{3,2,1,0:T(8,128)S(1)} %tmat_apply.3.own_ref.refs_3_), channel_id=1, source_target_pairs={{0,4},{2,6},{4,0},{6,2},{8,12},{10,14},{12,8},{14,10},{16,20},{18,... | collective-permute-start | bytes 393224 | tf_op jit(solution)/shard_map/ppermute | solution.py:460
  12.6 0.7 copy-start.2
  18.7 10.4 %collective-permute-start.4 = (f32[5,2,32,256]{3,2,1,0:T(8,128)S(1)}, f32[5,2,32,256]{3,2,1,0:T(8,128)S(1)}, u32[]{:S(2)}, u32[]{:S(2)}) collective-permute-start(f32[5,2,32,256]{3,2,1,0:T(8,128)S(1)} %get-tuple-element.41), channel_id=1, source_target_pairs={{0,2},{2,0},{4,6},{6,4},{8,10},{10,8},{12,14},{14,12},{16,18},{18,... | collective-permute-start | bytes 983048 | tf_op jit(solution)/shard_map/ppermute | solution.py:460
  18.8 10.3 %collective-permute-start.5 = (f32[5,2,32,256]{3,2,1,0:T(8,128)S(1)}, f32[5,2,32,256]{3,2,1,0:T(8,128)S(1)}, u32[]{:S(2)}, u32[]{:S(2)}) collective-permute-start(f32[5,2,32,256]{3,2,1,0:T(8,128)S(1)} %get-tuple-element.42), channel_id=1, source_target_pairs={{0,4},{2,6},{4,0},{6,2},{8,12},{10,14},{12,8},{14,10},{16,20},{18,... | collective-permute-start | bytes 983048 | tf_op jit(solution)/shard_map/ppermute | solution.py:460
  29.2 25.8 %collective-permute-start.6 = (f32[8,2,32,256]{3,2,1,0:T(8,128)S(1)}, f32[8,2,32,256]{3,2,1,0:T(8,128)S(1)}, u32[]{:S(2)}, u32[]{:S(2)}) collective-permute-start(f32[8,2,32,256]{3,2,1,0:T(8,128)S(1)} %get-tuple-element.46), channel_id=1, source_target_pairs={{0,2},{2,0},{4,6},{6,4},{8,10},{10,8},{12,14},{14,12},{16,18},{18,... | collective-permute-start | bytes 1572872 | tf_op jit(solution)/shard_map/ppermute | solution.py:460
  29.8 25.2 %collective-permute-start.7 = (f32[8,2,32,256]{3,2,1,0:T(8,128)S(1)}, f32[8,2,32,256]{3,2,1,0:T(8,128)S(1)}, u32[]{:S(2)}, u32[]{:S(2)}) collective-permute-start(f32[8,2,32,256]{3,2,1,0:T(8,128)S(1)} %get-tuple-element.47), channel_id=1, source_target_pairs={{0,4},{2,6},{4,0},{6,2},{8,12},{10,14},{12,8},{14,10},{16,20},{18,... | collective-permute-start | bytes 1572872 | tf_op jit(solution)/shard_map/ppermute | solution.py:460
  55.1 9.4 %collective-permute-start.8 = (f32[6,2,32,256]{3,2,1,0:T(8,128)S(1)}, f32[6,2,32,256]{3,2,1,0:T(8,128)S(1)}, u32[]{:S(2)}, u32[]{:S(2)}) collective-permute-start(f32[6,2,32,256]{3,2,1,0:T(8,128)S(1)} %get-tuple-element.49), channel_id=1, source_target_pairs={{0,2},{2,0},{4,6},{6,4},{8,10},{10,8},{12,14},{14,12},{16,18},{18,... | collective-permute-start | bytes 1179656 | tf_op jit(solution)/shard_map/ppermute | solution.py:460
  55.6 8.9 %collective-permute-start.9 = (f32[6,2,32,256]{3,2,1,0:T(8,128)S(1)}, f32[6,2,32,256]{3,2,1,0:T(8,128)S(1)}, u32[]{:S(2)}, u32[]{:S(2)}) collective-permute-start(f32[6,2,32,256]{3,2,1,0:T(8,128)S(1)} %get-tuple-element.50), channel_id=1, source_target_pairs={{0,4},{2,6},{4,0},{6,2},{8,12},{10,14},{12,8},{14,10},{16,20},{18,... | collective-permute-start | bytes 1179656 | tf_op jit(solution)/shard_map/ppermute | solution.py:460
  55.6 11.3 %collective-permute-start.12 = (f32[4,2,32,256]{3,2,1,0:T(8,128)S(1)}, f32[4,2,32,256]{3,2,1,0:T(8,128)S(1)}, u32[]{:S(2)}, u32[]{:S(2)}) collective-permute-start(f32[4,2,32,256]{3,2,1,0:T(8,128)S(1)} %get-tuple-element.55), channel_id=1, source_target_pairs={{0,8},{2,10},{4,12},{6,14},{8,0},{10,2},{12,4},{14,6},{16,24},{18,... | collective-permute-start | bytes 786440 | tf_op jit(solution)/shard_map/ppermute | solution.py:460
  64.5 8.7 %collective-permute-start.10 = (f32[3,2,32,256]{3,2,1,0:T(8,128)S(1)}, f32[3,2,32,256]{3,2,1,0:T(8,128)S(1)}, u32[]{:S(2)}, u32[]{:S(2)}) collective-permute-start(f32[3,2,32,256]{3,2,1,0:T(8,128)S(1)} %get-tuple-element.52), channel_id=1, source_target_pairs={{0,2},{2,0},{4,6},{6,4},{8,10},{10,8},{12,14},{14,12},{16,18},{18,... | collective-permute-start | bytes 589832 | tf_op jit(solution)/shard_map/ppermute | solution.py:460
  66.8 6.4 %collective-permute-start.11 = (f32[3,2,32,256]{3,2,1,0:T(8,128)S(1)}, f32[3,2,32,256]{3,2,1,0:T(8,128)S(1)}, u32[]{:S(2)}, u32[]{:S(2)}) collective-permute-start(f32[3,2,32,256]{3,2,1,0:T(8,128)S(1)} %get-tuple-element.53), channel_id=1, source_target_pairs={{0,4},{2,6},{4,0},{6,2},{8,12},{10,14},{12,8},{14,10},{16,20},{18,... | collective-permute-start | bytes 589832 | tf_op jit(solution)/shard_map/ppermute | solution.py:460
  66.9 9.9 %collective-permute-start.13 = (f32[2,2,32,256]{3,2,1,0:T(8,128)S(1)}, f32[2,2,32,256]{3,2,1,0:T(8,128)S(1)}, u32[]{:S(2)}, u32[]{:S(2)}) collective-permute-start(f32[2,2,32,256]{3,2,1,0:T(8,128)S(1)} %pack_sums.2.refs_5_), channel_id=1, source_target_pairs={{0,16},{2,18},{4,20},{6,22},{8,24},{10,26},{12,28},{14,30},{16,0},... | collective-permute-start | bytes 393224 | tf_op jit(solution)/shard_map/ppermute | solution.py:460
  76.8 1.6 %collective-permute-start.14 = (f32[2,2,32,512]{3,2,1,0:T(8,128)S(1)}, f32[2,2,32,512]{3,2,1,0:T(8,128)S(1)}, u32[]{:S(2)}, u32[]{:S(2)}) collective-permute-start(f32[2,2,32,512]{3,2,1,0:T(8,128)S(1)} %total.2.mine_ref), channel_id=1, source_target_pairs={{0,1},{1,0},{2,3},{3,2},{4,5},{5,4},{6,7},{7,6},{8,9},{9,8},{10,11... | collective-permute-start | bytes 786440 | tf_op jit(solution)/shard_map/ppermute | solution.py:455
  79.3 1.4 collective-permute-start.15
  79.5 5.8 %collective-permute-start.16 = (f32[2,2,32,256]{3,2,1,0:T(8,128)S(1)}, f32[2,2,32,256]{3,2,1,0:T(8,128)S(1)}, u32[]{:S(2)}, u32[]{:S(2)}) collective-permute-start(f32[2,2,32,256]{3,2,1,0:T(8,128)S(1)} %tmat_apply.4.own_ref.refs_3_), channel_id=1, source_target_pairs={{0,2},{2,0},{4,6},{6,4},{8,10},{10,8},{12,14},{14,12},{16,18},{18,... | collective-permute-start | bytes 393224 | tf_op jit(solution)/shard_map/ppermute | solution.py:460
  79.5 5.8 %collective-permute-start.17 = (f32[2,2,32,256]{3,2,1,0:T(8,128)S(1)}, f32[2,2,32,256]{3,2,1,0:T(8,128)S(1)}, u32[]{:S(2)}, u32[]{:S(2)}) collective-permute-start(f32[2,2,32,256]{3,2,1,0:T(8,128)S(1)} %tmat_apply.4.own_ref.refs_3_), channel_id=1, source_target_pairs={{0,4},{2,6},{4,0},{6,2},{8,12},{10,14},{12,8},{14,10},{16,20},{18,... | collective-permute-start | bytes 393224 | tf_op jit(solution)/shard_map/ppermute | solution.py:460
  85.3 9.2 %collective-permute-start.18 = (f32[5,2,32,256]{3,2,1,0:T(8,128)S(1)}, f32[5,2,32,256]{3,2,1,0:T(8,128)S(1)}, u32[]{:S(2)}, u32[]{:S(2)}) collective-permute-start(f32[5,2,32,256]{3,2,1,0:T(8,128)S(1)} %get-tuple-element.56), channel_id=1, source_target_pairs={{0,2},{2,0},{4,6},{6,4},{8,10},{10,8},{12,14},{14,12},{16,18},{18,... | collective-permute-start | bytes 983048 | tf_op jit(solution)/shard_map/ppermute | solution.py:460
  87.1 8.6 %collective-permute-start.19 = (f32[5,2,32,256]{3,2,1,0:T(8,128)S(1)}, f32[5,2,32,256]{3,2,1,0:T(8,128)S(1)}, u32[]{:S(2)}, u32[]{:S(2)}) collective-permute-start(f32[5,2,32,256]{3,2,1,0:T(8,128)S(1)} %get-tuple-element.57), channel_id=1, source_target_pairs={{0,4},{2,6},{4,0},{6,2},{8,12},{10,14},{12,8},{14,10},{16,20},{18,... | collective-permute-start | bytes 983048 | tf_op jit(solution)/shard_map/ppermute | solution.py:460
  95.8 23.5 %collective-permute-start.20 = (f32[8,2,32,256]{3,2,1,0:T(8,128)S(1)}, f32[8,2,32,256]{3,2,1,0:T(8,128)S(1)}, u32[]{:S(2)}, u32[]{:S(2)}) collective-permute-start(f32[8,2,32,256]{3,2,1,0:T(8,128)S(1)} %get-tuple-element.59), channel_id=1, source_target_pairs={{0,2},{2,0},{4,6},{6,4},{8,10},{10,8},{12,14},{14,12},{16,18},{18,... | collective-permute-start | bytes 1572872 | tf_op jit(solution)/shard_map/ppermute | solution.py:460
  96.5 22.8 %collective-permute-start.21 = (f32[8,2,32,256]{3,2,1,0:T(8,128)S(1)}, f32[8,2,32,256]{3,2,1,0:T(8,128)S(1)}, u32[]{:S(2)}, u32[]{:S(2)}) collective-permute-start(f32[8,2,32,256]{3,2,1,0:T(8,128)S(1)} %get-tuple-element.60), channel_id=1, source_target_pairs={{0,4},{2,6},{4,0},{6,2},{8,12},{10,14},{12,8},{14,10},{16,20},{18,... | collective-permute-start | bytes 1572872 | tf_op jit(solution)/shard_map/ppermute | solution.py:460
  119.4 9.9 %collective-permute-start.22 = (f32[6,2,32,256]{3,2,1,0:T(8,128)S(1)}, f32[6,2,32,256]{3,2,1,0:T(8,128)S(1)}, u32[]{:S(2)}, u32[]{:S(2)}) collective-permute-start(f32[6,2,32,256]{3,2,1,0:T(8,128)S(1)} %get-tuple-element.61), channel_id=1, source_target_pairs={{0,2},{2,0},{4,6},{6,4},{8,10},{10,8},{12,14},{14,12},{16,18},{18,... | collective-permute-start | bytes 1179656 | tf_op jit(solution)/shard_map/ppermute | solution.py:460
  120.2 9.2 %collective-permute-start.23 = (f32[6,2,32,256]{3,2,1,0:T(8,128)S(1)}, f32[6,2,32,256]{3,2,1,0:T(8,128)S(1)}, u32[]{:S(2)}, u32[]{:S(2)}) collective-permute-start(f32[6,2,32,256]{3,2,1,0:T(8,128)S(1)} %get-tuple-element.62), channel_id=1, source_target_pairs={{0,4},{2,6},{4,0},{6,2},{8,12},{10,14},{12,8},{14,10},{16,20},{18,... | collective-permute-start | bytes 1179656 | tf_op jit(solution)/shard_map/ppermute | solution.py:460
  120.2 11.6 %collective-permute-start.26 = (f32[4,2,32,256]{3,2,1,0:T(8,128)S(1)}, f32[4,2,32,256]{3,2,1,0:T(8,128)S(1)}, u32[]{:S(2)}, u32[]{:S(2)}) collective-permute-start(f32[4,2,32,256]{3,2,1,0:T(8,128)S(1)} %get-tuple-element.67), channel_id=1, source_target_pairs={{0,8},{2,10},{4,12},{6,14},{8,0},{10,2},{12,4},{14,6},{16,24},{18,... | collective-permute-start | bytes 786440 | tf_op jit(solution)/shard_map/ppermute | solution.py:460
  129.4 8.0 %collective-permute-start.24 = (f32[3,2,32,256]{3,2,1,0:T(8,128)S(1)}, f32[3,2,32,256]{3,2,1,0:T(8,128)S(1)}, u32[]{:S(2)}, u32[]{:S(2)}) collective-permute-start(f32[3,2,32,256]{3,2,1,0:T(8,128)S(1)} %get-tuple-element.64), channel_id=1, source_target_pairs={{0,2},{2,0},{4,6},{6,4},{8,10},{10,8},{12,14},{14,12},{16,18},{18,... | collective-permute-start | bytes 589832 | tf_op jit(solution)/shard_map/ppermute | solution.py:460
  131.5 6.0 %collective-permute-start.25 = (f32[3,2,32,256]{3,2,1,0:T(8,128)S(1)}, f32[3,2,32,256]{3,2,1,0:T(8,128)S(1)}, u32[]{:S(2)}, u32[]{:S(2)}) collective-permute-start(f32[3,2,32,256]{3,2,1,0:T(8,128)S(1)} %get-tuple-element.65), channel_id=1, source_target_pairs={{0,4},{2,6},{4,0},{6,2},{8,12},{10,14},{12,8},{14,10},{16,20},{18,... | collective-permute-start | bytes 589832 | tf_op jit(solution)/shard_map/ppermute | solution.py:460
  131.8 9.2 %collective-permute-start.27 = (f32[2,2,32,256]{3,2,1,0:T(8,128)S(1)}, f32[2,2,32,256]{3,2,1,0:T(8,128)S(1)}, u32[]{:S(2)}, u32[]{:S(2)}) collective-permute-start(f32[2,2,32,256]{3,2,1,0:T(8,128)S(1)} %pack_sums.3.refs_5_), channel_id=1, source_target_pairs={{0,16},{2,18},{4,20},{6,22},{8,24},{10,26},{12,28},{14,30},{16,0},... | collective-permute-start | bytes 393224 | tf_op jit(solution)/shard_map/ppermute | solution.py:460
  141.0 1.6 %collective-permute-start.28 = (f32[2,2,32,512]{3,2,1,0:T(8,128)S(1)}, f32[2,2,32,512]{3,2,1,0:T(8,128)S(1)}, u32[]{:S(2)}, u32[]{:S(2)}) collective-permute-start(f32[2,2,32,512]{3,2,1,0:T(8,128)S(1)} %total.3.mine_ref), channel_id=1, source_target_pairs={{0,1},{1,0},{2,3},{3,2},{4,5},{5,4},{6,7},{7,6},{8,9},{9,8},{10,11... | collective-permute-start | bytes 786440 | tf_op jit(solution)/shard_map/ppermute | solution.py:455
  (1 other events, 0.7 us)

commit v2 on v0

--- a/solution.py
+++ b/solution.py
@@ -542,13 +542,12 @@
 
     def summed(layer, particle, arrived):
         terms = [(number, row_of(particle, layer)) for number in range(3)]
-        for step in range(arrived):
-            terms.append((3 + step, (layer >> (step + 1)) * particles + particle))
-        return terms
+        return terms + [(3 + step, layer * particles + particle) for step in range(arrived)]
 
     def half_sums(bit, arrived):
-        chosen = range(bit, layers, 2 * bit)
-        return [summed(layer, particle, arrived) for layer in chosen for particle in every]
+        return [
+            summed(layer, particle, arrived) for layer in range(bit, 2 * bit) for particle in every
+        ]
 
     inputs = [products_o, x3, y3] + reached
     tails = []
@@ -559,11 +558,11 @@
     x4, y4, sums, mark = pack(
         "pack_fourth",
         inputs,
-        [tails, tails, half_sums(1, 0), [[(1, 0)]]],
+        [tails, tails, half_sums(powers[-1], 0), [[(1, 0)]]],
         [near],
     )
     x4, y4 = across(x4, 1), across(y4, 2)
-    arrived = [across(sums, COLUMNS)]
+    arrived = [across(sums, powers[-1] * COLUMNS)]
     copies = []
     for particle in every:
         for layer in rest:
@@ -585,22 +584,22 @@
         [near],
     )
     x5, y5 = across(x5, 1), across(y5, 2)
-    for bit in powers[1:]:
-        inputs = [products_o, x3, y3] + arrived
-        (sums,) = pack("pack_sums", inputs, [half_sums(bit, len(arrived))], [mark])
-        arrived.append(across(sums, bit * COLUMNS))
     copies = []
     for particle in every:
         for layer in rest:
             copies.append((0, tail(particle, layer), at(1, particle, layer)))
             copies.append((1, tail(particle, layer), at(2, particle, layer)))
-    near = forward((3,), index, [x4, y4], tuple(copies), parts, *sizes, near, False, [mark, sums])
+    near = forward((3,), index, [x4, y4], tuple(copies), parts, *sizes, near, False, [mark])
+    for bit in powers[-2::-1]:
+        inputs = [products_o, x3, y3] + arrived
+        (sums,) = pack("pack_sums", inputs, [half_sums(bit, len(arrived))], [near])
+        arrived.append(across(sums, bit * COLUMNS))
     copies = []
     for number, group in ((0, by_y), (1, by_x)):
         for order, particle in enumerate(group):
             for layer in rest:
                 copies.append((number, tail(order, layer), at(3, particle, layer)))
-    near = forward((4,), index, [x5, y5], tuple(copies), parts, *sizes, near, True, [])
+    near = forward((4,), index, [x5, y5], tuple(copies), parts, *sizes, near, True, [sums])
     halves = [(products_o, layers), (x3, layers), (y3, layers)] + [(value, 1) for value in arrived]
     return whole_total(side, incident, [near], halves), parts
 

time: 126 us -> 125 us (level)
  starting transfers between devices: 43.8 us -> 33.6 us
  Pallas kernels: 59.8 us -> 67.6 us
    ppermute x30, starting transfers between devices: 42.9 us -> 32.6 us  [across(): lax.ppermute(value, 'owner', [(source, source ^ bit) for source in range(...]
    pallas_call x6, Pallas kernels: 25.7 us -> 29.8 us  [backward(): pl.pallas_call(functools.partial(backward_kernel, first, groups, base), o...]
    pallas_call x8, Pallas kernels: 27.7 us -> 31.2 us  [forward(): pl.pallas_call(functools.partial(forward_kernel, groups, copies, len(fiel...]
  transfers between devices with their start and end apart: 35 -> 35, of which waited for: 13 -> 14; matrix products, arithmetic and copies ran while one was open for 0% -> 0% of each run, Pallas kernels for 44% -> 51%
where the time goes in v2:
time: 125 us; the launch traced here: 124 us
  Pallas kernels  67.6 us (54%)
  starting transfers between devices  33.6 us (27%)
  waiting for transfers between devices  17.3 us (14%)
  local copies, waits for them, and re-layouts  3.85 us (3%)
  between operations  1.68 us (1%)
    ppermute x30, starting transfers between devices, across(): lax.ppermute(value, 'owner', [(source, source ^ bit) for source in range(...  32.6 us
    pallas_call x8, Pallas kernels, forward(): pl.pallas_call(functools.partial(forward_kernel, groups, copies, len(fiel...  31.2 us
    pallas_call x6, Pallas kernels, backward(): pl.pallas_call(functools.partial(backward_kernel, first, groups, base), o...  29.8 us
    ppermute x30, waiting for transfers between devices, across(): lax.ppermute(value, 'owner', [(source, source ^ bit) for source in range(...  14.3 us
    unnamed x8, local copies, waits for them, and re-layouts  3.85 us
    pallas_call x3, Pallas kernels, apply_tmat(): pl.pallas_call(functools.partial(tmat_kernel, halves), out_shape=[half_sh...  3.31 us
    ppermute x5, waiting for transfers between devices, from_other(): return lax.ppermute(value, 'pair', [(0, 1), (1, 0)])  3.05 us
  transfers between devices with their start and end apart: 35, of which 14 were waited for; matrix products, arithmetic and copies ran while one was open for 0% of the time, Pallas kernels for 51%

profile of v2, /device:TPU:0, one launch (start us, length us, event | category | flops | bytes accessed | tf_op | source)
XLA Modules:
  0.0 124.1 jit_solution(7778425226956855546)
XLA Ops:
  1.8 1.8 %slot_index.1.after_ref.index_ref = s32[321]{0:T(512)} custom-call(s32[1]{0:T(128)} %bitcast.1.owner_ref, s32[1]{0:T(128)} %bitcast.side_ref, s32[336]{0:T(512)} %partners_ref.1, s32[32]{0:T(128)} %rows_of_ref.1, s32[21]{0:T(128)} %holders_ref.1, s32[1]{0:T(128)S(6)} %copy.13.live_ref), custom_call_target="tpu_custom_call" | custom-call | tf_op jit(solution)/shard_map/slot_index/pallas_call | solution.py:92
  3.6 1.6 %copy-done = f32[2,2,256,512]{3,2,1,0:T(8,128)S(1)} copy-done((f32[2,2,256,512]{3,2,1,0:T(8,128)S(1)}, f32[2,2,256,512]{3,2,1,0:T(8,128)}, u32[]{:S(2)}) %copy-start) | copy-done | bytes 2097176
  8.5 2.9 %collective-permute-start.4 = (f32[2,2,32,256]{3,2,1,0:T(8,128)S(1)}, f32[2,2,32,256]{3,2,1,0:T(8,128)S(1)}, u32[]{:S(2)}, u32[]{:S(2)}) collective-permute-start(f32[2,2,32,256]{3,2,1,0:T(8,128)S(1)} %tmat_apply.3.own_ref.refs_3_), channel_id=1, source_target_pairs={{0,8},{2,10},{4,12},{6,14},{8,0},{10,2},{12,4},{14,6},{16,24},{18,... | collective-permute-start | bytes 393224 | tf_op jit(solution)/shard_map/ppermute | solution.py:451
  12.8 1.6 %collective-permute-start.2 = (f32[2,2,32,256]{3,2,1,0:T(8,128)S(1)}, f32[2,2,32,256]{3,2,1,0:T(8,128)S(1)}, u32[]{:S(2)}, u32[]{:S(2)}) collective-permute-start(f32[2,2,32,256]{3,2,1,0:T(8,128)S(1)} %tmat_apply.3.own_ref.refs_3_), channel_id=1, source_target_pairs={{0,2},{2,0},{4,6},{6,4},{8,10},{10,8},{12,14},{14,12},{16,18},{18,... | collective-permute-start | bytes 393224 | tf_op jit(solution)/shard_map/ppermute | solution.py:451
  15.1 4.5 %backward_group2.2 = (f32[8,2,32,256]{3,2,1,0:T(8,128)S(1)}, bf16[21,2,2,512,256]{4,3,2,1,0:T(8,128)(2,1)}) custom-call(s32[321]{0:T(512)S(1)} %copy-done.2, f32[2,2,32,256]{3,2,1,0:T(8,128)S(1)} %tmat_apply.3.own_ref.refs_3_, f32[2,2,32,256]{3,2,1,0:T(8,128)S(1)} %collective-permute-done.1.other_ref, f32[21,2,512,256]{3,2,1,0:T(8,128)} %blocks_ref.5), custom_call_target="tpu_custom_call" | custom-call | flops 4194304 | bytes 131072 | tf_op jit(solution)/shard_map/backward_group2/pallas_call | solution.py:300
  19.8 1.8 %collective-permute-start.6 = (f32[5,2,32,256]{3,2,1,0:T(8,128)S(1)}, f32[5,2,32,256]{3,2,1,0:T(8,128)S(1)}, u32[]{:S(2)}, u32[]{:S(2)}) collective-permute-start(f32[5,2,32,256]{3,2,1,0:T(8,128)S(1)} %get-tuple-element.46), channel_id=1, source_target_pairs={{0,4},{2,6},{4,0},{6,2},{8,12},{10,14},{12,8},{14,10},{16,20},{18,... | collective-permute-start | bytes 983048 | tf_op jit(solution)/shard_map/ppermute | solution.py:451
  23.0 7.6 %backward_group1.2 = (f32[16,2,32,256]{3,2,1,0:T(8,128)S(1)}, bf16[21,2,2,512,256]{4,3,2,1,0:T(8,128)(2,1)}) custom-call(s32[321]{0:T(512)S(1)} %copy-done.2, f32[2,2,32,256]{3,2,1,0:T(8,128)S(1)} %tmat_apply.3.own_ref.refs_3_, f32[2,2,32,256]{3,2,1,0:T(8,128)S(1)} %collective-permute-done.1.other_ref, ...), custom_call_target="tpu_custom_call", output_to_operand_aliasing={{1}: (4, {})} | custom-call | flops 4194304 | bytes 131072 | tf_op jit(solution)/shard_map/backward_group1/pallas_call | solution.py:300
  30.9 4.3 %collective-permute-start.9 = (f32[8,2,32,256]{3,2,1,0:T(8,128)S(1)}, f32[8,2,32,256]{3,2,1,0:T(8,128)S(1)}, u32[]{:S(2)}, u32[]{:S(2)}) collective-permute-start(f32[8,2,32,256]{3,2,1,0:T(8,128)S(1)} %get-tuple-element.52), channel_id=1, source_target_pairs={{0,4},{2,6},{4,0},{6,2},{8,12},{10,14},{12,8},{14,10},{16,20},{18,... | collective-permute-start | bytes 1572872 | tf_op jit(solution)/shard_map/ppermute | solution.py:451
  35.2 6.0 %backward_group0.2 = (f32[8,2,32,256]{3,2,1,0:T(8,128)S(1)}, bf16[21,2,2,512,256]{4,3,2,1,0:T(8,128)(2,1)}) custom-call(s32[321]{0:T(512)S(1)} %copy-done.2, f32[2,2,32,256]{3,2,1,0:T(8,128)S(1)} %get-tuple-element.48.own_ref, f32[2,2,32,256]{3,2,1,0:T(8,128)S(1)} %collective-permute-done.1.other_ref, ...), custom_call_target="tpu_custom_call", output_to_operand_aliasing={{1}: (4, {})} | custom-call | flops 4194304 | bytes 131072 | tf_op jit(solution)/shard_map/backward_group0/pallas_call | solution.py:300
  41.2 3.6 %forward_group1.2.refs_6_.refs_4_ = f32[2,512,128]{2,1,0:T(8,128)S(1)} custom-call(s32[321]{0:T(512)S(1)} %copy-done.2, f32[2,2,32,256]{3,2,1,0:T(8,128)S(1)} %collective-permute-done.2.refs_1_.refs_0_, f32[2,2,32,256]{3,2,1,0:T(8,128)S(1)} %collective-permute-done.3.refs_2_.refs_1_, f32[5,2,32,256]{3,2,1,0:T(8,128)S(1)} %collective-permute-done.5.refs_1_.refs_2_, ...), custom_call_target="tpu_custom_call" | custom-call | flops 4194304 | bytes 524288 | tf_op jit(solution)/shard_map/forward_group1/pallas_call | solution.py:378
  45.9 1.9 %collective-permute-start.12 = (f32[6,2,32,256]{3,2,1,0:T(8,128)S(1)}, f32[6,2,32,256]{3,2,1,0:T(8,128)S(1)}, u32[]{:S(2)}, u32[]{:S(2)}) collective-permute-start(f32[6,2,32,256]{3,2,1,0:T(8,128)S(1)} %get-tuple-element.56), channel_id=1, source_target_pairs={{0,4},{2,6},{4,0},{6,2},{8,12},{10,14},{12,8},{14,10},{16,20},{18,... | collective-permute-start | bytes 1179656 | tf_op jit(solution)/shard_map/ppermute | solution.py:451
  47.9 4.5 %forward_group0.2.refs_2_.refs_3_ = f32[2,512,128]{2,1,0:T(8,128)S(1)} custom-call(s32[321]{0:T(512)S(1)} %copy-done.2, f32[2,2,32,256]{3,2,1,0:T(8,128)S(1)} %collective-permute-done.4.refs_4_.refs_3_.refs_0_, f32[2,2,32,256]{3,2,1,0:T(8,128)S(1)} %collective-permute-done.7.refs_5_.refs_4_.refs_1_, ...), custom_call_target="tpu_custom_call" | custom-call | flops 4194304 | bytes 524288 | tf_op jit(solution)/shard_map/forward_group0/pallas_call | solution.py:378
  52.4 2.0 %collective-permute-done.11.refs_0_ = f32[6,2,32,256]{3,2,1,0:T(8,128)S(1)} collective-permute-done((f32[6,2,32,256]{3,2,1,0:T(8,128)S(1)}, f32[6,2,32,256]{3,2,1,0:T(8,128)S(1)}, u32[]{:S(2)}, u32[]{:S(2)}) %collective-permute-start.11) | collective-permute-done | bytes 393248 | tf_op jit(solution)/shard_map/ppermute | solution.py:451
  54.4 1.8 %collective-permute-start.13 = (f32[3,2,32,256]{3,2,1,0:T(8,128)S(1)}, f32[3,2,32,256]{3,2,1,0:T(8,128)S(1)}, u32[]{:S(2)}, u32[]{:S(2)}) collective-permute-start(f32[3,2,32,256]{3,2,1,0:T(8,128)S(1)} %get-tuple-element.58), channel_id=1, source_target_pairs={{0,2},{2,0},{4,6},{6,4},{8,10},{10,8},{12,14},{14,12},{16,18},{18,... | collective-permute-start | bytes 589832 | tf_op jit(solution)/shard_map/ppermute | solution.py:451
  57.6 4.5 %forward_group3.2.refs_4_.refs_3_ = f32[2,512,128]{2,1,0:T(8,128)S(1)} custom-call(s32[321]{0:T(512)S(1)} %copy-done.2, f32[6,2,32,256]{3,2,1,0:T(8,128)S(1)} %collective-permute-done.11.refs_0_, f32[6,2,32,256]{3,2,1,0:T(8,128)S(1)} %collective-permute-done.12.refs_1_, bf16[21,2,2,512,256]{4,3,2,1,0:T(8,128)(2,1)} %get-tuple-element.54.refs_4_.refs_3_.refs_2_.blocks_ref, ...), custom_call_target="tpu_custom_call" | custom-call | flops 4194304 | bytes 524288 | tf_op jit(solution)/shard_map/forward_group3/pallas_call | solution.py:378
  62.3 3.0 %forward_group4.2.refs_0_ = f32[2,2,32,512]{3,2,1,0:T(8,128)S(1)} custom-call(s32[321]{0:T(512)S(1)} %copy-done.2, f32[3,2,32,256]{3,2,1,0:T(8,128)S(1)} %collective-permute-done.13.refs_0_, f32[3,2,32,256]{3,2,1,0:T(8,128)S(1)} %collective-permute-done.14.refs_1_, bf16[21,2,2,512,256]{4,3,2,1,0:T(8,128)(2,1)} %get-tuple-element.54.refs_4_.refs_3_.refs_2_.blocks_ref, ...), custom_call_target="tpu_custom_call" | custom-call | flops 4194304 | bytes 262144 | tf_op jit(solution)/shard_map/forward_group4/pallas_call | solution.py:378
  65.3 1.9 %collective-permute-done.16.refs_5_ = f32[2,2,32,256]{3,2,1,0:T(8,128)S(1)} collective-permute-done((f32[2,2,32,256]{3,2,1,0:T(8,128)S(1)}, f32[2,2,32,256]{3,2,1,0:T(8,128)S(1)}, u32[]{:S(2)}, u32[]{:S(2)}) %collective-permute-start.16) | collective-permute-done | bytes 131104 | tf_op jit(solution)/shard_map/ppermute | solution.py:451
  71.3 3.1 %backward_group2.3.refs_0_ = f32[8,2,32,256]{3,2,1,0:T(8,128)S(1)} custom-call(s32[321]{0:T(512)S(1)} %copy-done.2, f32[2,2,32,256]{3,2,1,0:T(8,128)S(1)} %tmat_apply.4.own_ref.refs_3_, f32[2,2,32,256]{3,2,1,0:T(8,128)S(1)} %collective-permute-done.18.other_ref, bf16[21,2,2,512,256]{4,3,2,1,0:T(8,128)(2,1)} %get-tuple-element.54.refs_4_.refs_3_.refs_2_.blocks_ref), custom_call_target="tpu_custom_call" | custom-call | flops 4194304 | bytes 131072 | tf_op jit(solution)/shard_map/backward_group2/pallas_call | solution.py:300
  77.9 2.2 %collective-permute-start.24 = (f32[2,2,32,256]{3,2,1,0:T(8,128)S(1)}, f32[2,2,32,256]{3,2,1,0:T(8,128)S(1)}, u32[]{:S(2)}, u32[]{:S(2)}) collective-permute-start(f32[2,2,32,256]{3,2,1,0:T(8,128)S(1)} %get-tuple-element.64), channel_id=1, source_target_pairs={{0,16},{2,18},{4,20},{6,22},{8,24},{10,26},{12,28},{14,30},{16,0},... | collective-permute-start | bytes 393224 | tf_op jit(solution)/shard_map/ppermute | solution.py:451
  80.1 4.6 %backward_group1.3.refs_0_ = f32[16,2,32,256]{3,2,1,0:T(8,128)S(1)} custom-call(s32[321]{0:T(512)S(1)} %copy-done.2, f32[2,2,32,256]{3,2,1,0:T(8,128)S(1)} %tmat_apply.4.own_ref.refs_3_, f32[2,2,32,256]{3,2,1,0:T(8,128)S(1)} %collective-permute-done.18.other_ref, bf16[21,2,2,512,256]{4,3,2,1,0:T(8,128)(2,1)} %get-tuple-element.54.refs_4_.refs_3_.refs_2_.blocks_ref), custom_call_target="tpu_custom_call" | custom-call | flops 4194304 | bytes 131072 | tf_op jit(solution)/shard_map/backward_group1/pallas_call | solution.py:300
  84.7 1.5 %collective-permute-done.24.refs_5_.refs_4_.refs_1_ = f32[2,2,32,256]{3,2,1,0:T(8,128)S(1)} collective-permute-done((f32[2,2,32,256]{3,2,1,0:T(8,128)S(1)}, f32[2,2,32,256]{3,2,1,0:T(8,128)S(1)}, u32[]{:S(2)}, u32[]{:S(2)}) %collective-permute-start.24) | collective-permute-done | bytes 131104 | tf_op jit(solution)/shard_map/ppermute | solution.py:451
  88.4 1.8 %collective-permute-start.27 = (f32[2,2,32,256]{3,2,1,0:T(8,128)S(1)}, f32[2,2,32,256]{3,2,1,0:T(8,128)S(1)}, u32[]{:S(2)}, u32[]{:S(2)}) collective-permute-start(f32[2,2,32,256]{3,2,1,0:T(8,128)S(1)} %get-tuple-element.68), channel_id=1, source_target_pairs={{0,16},{2,18},{4,20},{6,22},{8,24},{10,26},{12,28},{14,30},{16,0},... | collective-permute-start | bytes 393224 | tf_op jit(solution)/shard_map/ppermute | solution.py:451
  90.2 4.0 %backward_group0.3.refs_5_.refs_0_.refs_1_ = f32[8,2,32,256]{3,2,1,0:T(8,128)S(1)} custom-call(s32[321]{0:T(512)S(1)} %copy-done.2, f32[2,2,32,256]{3,2,1,0:T(8,128)S(1)} %get-tuple-element.65.own_ref, f32[2,2,32,256]{3,2,1,0:T(8,128)S(1)} %collective-permute-done.18.other_ref, bf16[21,2,2,512,256]{4,3,2,1,0:T(8,128)(2,1)} %get-tuple-element.54.refs_4_.refs_3_.refs_2_.blocks_ref), custom_call_target="tpu_custom_call" | custom-call | flops 4194304 | bytes 131072 | tf_op jit(solution)/shard_map/backward_group0/pallas_call | solution.py:300
  94.2 3.6 %forward_group1.3.refs_6_.refs_4_ = f32[2,512,128]{2,1,0:T(8,128)S(1)} custom-call(s32[321]{0:T(512)S(1)} %copy-done.2, f32[2,2,32,256]{3,2,1,0:T(8,128)S(1)} %collective-permute-done.19.refs_1_.refs_0_, f32[2,2,32,256]{3,2,1,0:T(8,128)S(1)} %collective-permute-done.20.refs_2_.refs_1_, f32[5,2,32,256]{3,2,1,0:T(8,128)S(1)} %collective-permute-done.22.refs_1_.refs_2_, ...), custom_call_target="tpu_custom_call" | custom-call | flops 4194304 | bytes 524288 | tf_op jit(solution)/shard_map/forward_group1/pallas_call | solution.py:378
  97.8 1.7 %collective-permute-done.25.refs_1_.refs_2_ = f32[8,2,32,256]{3,2,1,0:T(8,128)S(1)} collective-permute-done((f32[8,2,32,256]{3,2,1,0:T(8,128)S(1)}, f32[8,2,32,256]{3,2,1,0:T(8,128)S(1)}, u32[]{:S(2)}, u32[]{:S(2)}) %collective-permute-start.25) | collective-permute-done | bytes 524320 | tf_op jit(solution)/shard_map/ppermute | solution.py:451
  99.7 1.7 %collective-permute-start.28 = (f32[6,2,32,256]{3,2,1,0:T(8,128)S(1)}, f32[6,2,32,256]{3,2,1,0:T(8,128)S(1)}, u32[]{:S(2)}, u32[]{:S(2)}) collective-permute-start(f32[6,2,32,256]{3,2,1,0:T(8,128)S(1)} %get-tuple-element.69), channel_id=1, source_target_pairs={{0,2},{2,0},{4,6},{6,4},{8,10},{10,8},{12,14},{14,12},{16,18},{18,... | collective-permute-start | bytes 1179656 | tf_op jit(solution)/shard_map/ppermute | solution.py:451
  102.6 4.5 %forward_group0.3.refs_2_.refs_3_ = f32[2,512,128]{2,1,0:T(8,128)S(1)} custom-call(s32[321]{0:T(512)S(1)} %copy-done.2, f32[2,2,32,256]{3,2,1,0:T(8,128)S(1)} %collective-permute-done.21.refs_4_.refs_3_.refs_0_, f32[2,2,32,256]{3,2,1,0:T(8,128)S(1)} %collective-permute-done.24.refs_5_.refs_4_.refs_1_, ...), custom_call_target="tpu_custom_call" | custom-call | flops 4194304 | bytes 524288 | tf_op jit(solution)/shard_map/forward_group0/pallas_call | solution.py:378
  107.1 2.1 %collective-permute-done.28.refs_0_ = f32[6,2,32,256]{3,2,1,0:T(8,128)S(1)} collective-permute-done((f32[6,2,32,256]{3,2,1,0:T(8,128)S(1)}, f32[6,2,32,256]{3,2,1,0:T(8,128)S(1)}, u32[]{:S(2)}, u32[]{:S(2)}) %collective-permute-start.28) | collective-permute-done | bytes 393248 | tf_op jit(solution)/shard_map/ppermute | solution.py:451
  111.3 4.5 %forward_group3.3.refs_4_.refs_3_ = f32[2,512,128]{2,1,0:T(8,128)S(1)} custom-call(s32[321]{0:T(512)S(1)} %copy-done.2, f32[6,2,32,256]{3,2,1,0:T(8,128)S(1)} %collective-permute-done.28.refs_0_, f32[6,2,32,256]{3,2,1,0:T(8,128)S(1)} %collective-permute-done.29.refs_1_, bf16[21,2,2,512,256]{4,3,2,1,0:T(8,128)(2,1)} %get-tuple-element.54.refs_4_.refs_3_.refs_2_.blocks_ref, ...), custom_call_target="tpu_custom_call" | custom-call | flops 4194304 | bytes 524288 | tf_op jit(solution)/shard_map/forward_group3/pallas_call | solution.py:378
  116.7 3.0 %forward_group4.3.refs_0_ = f32[2,2,32,512]{3,2,1,0:T(8,128)S(1)} custom-call(s32[321]{0:T(512)S(1)} %copy-done.2, f32[3,2,32,256]{3,2,1,0:T(8,128)S(1)} %collective-permute-done.30.refs_0_, f32[3,2,32,256]{3,2,1,0:T(8,128)S(1)} %collective-permute-done.31.refs_1_, bf16[21,2,2,512,256]{4,3,2,1,0:T(8,128)(2,1)} %get-tuple-element.54.refs_4_.refs_3_.refs_2_.blocks_ref, ...), custom_call_target="tpu_custom_call" | custom-call | flops 4194304 | bytes 262144 | tf_op jit(solution)/shard_map/forward_group4/pallas_call | solution.py:378
  121.0 1.5 %collective-permute-done.34.theirs_ref = f32[2,2,32,512]{3,2,1,0:T(8,128)S(1)} collective-permute-done((f32[2,2,32,512]{3,2,1,0:T(8,128)S(1)}, f32[2,2,32,512]{3,2,1,0:T(8,128)S(1)}, u32[]{:S(2)}, u32[]{:S(2)}) %collective-permute-start.34) | collective-permute-done | bytes 262176 | tf_op jit(solution)/shard_map/ppermute | solution.py:446
  122.5 1.5 %tmat_apply.5 = (f32[2,2,32,256]{3,2,1,0:T(8,128)}, f32[2,2,32,256]{3,2,1,0:T(8,128)}) custom-call(s32[1]{0:T(128)} %bitcast.side_ref, f32[2,2,32,512]{3,2,1,0:T(8,128)S(1)} %total.3.mine_ref, f32[2,2,32,512]{3,2,1,0:T(8,128)S(1)} %collective-permute-done.34.theirs_ref, bf16[2,256,2048]{2,1,0:T(8,128)(2,1)S(1)} %get-tuple-element.41.parts_ref), custom_call_target="tpu_custom_call" | custom-call | tf_op jit(solution)/shard_map/tmat_apply/pallas_call | solution.py:171
  (77 shorter events, 25.6 us)
Async XLA Ops:
  0.6 6.9 %collective-permute-start = (f32[2,2,32,256]{3,2,1,0:T(8,128)}, f32[2,2,32,256]{3,2,1,0:T(8,128)S(1)}, u32[]{:S(2)}, u32[]{:S(2)}) collective-permute-start(f32[2,2,32,256]{3,2,1,0:T(8,128)} %incident_ref.1), channel_id=1, source_target_pairs={{0,1},{1,0},{2,3},{3,2},{4,5},{5,4},{6,7},{7,6},{8,9},{9,8},{10,11... | collective-permute-start | bytes 393224 | tf_op jit(solution)/shard_map/ppermute | solution.py:446
  8.4 6.0 %collective-permute-start.1 = (f32[2,2,32,256]{3,2,1,0:T(8,128)S(1)}, f32[2,2,32,256]{3,2,1,0:T(8,128)S(1)}, u32[]{:S(2)}, u32[]{:S(2)}) collective-permute-start(f32[2,2,32,256]{3,2,1,0:T(8,128)S(1)} %tmat_apply.3.own_ref.refs_3_), channel_id=1, source_target_pairs={{0,1},{1,0},{2,3},{3,2},{4,5},{5,4},{6,7},{7,6},{8,9},{9,8},{10,11... | collective-permute-start | bytes 393224 | tf_op jit(solution)/shard_map/ppermute | solution.py:446
  8.5 11.1 %collective-permute-start.4 = (f32[2,2,32,256]{3,2,1,0:T(8,128)S(1)}, f32[2,2,32,256]{3,2,1,0:T(8,128)S(1)}, u32[]{:S(2)}, u32[]{:S(2)}) collective-permute-start(f32[2,2,32,256]{3,2,1,0:T(8,128)S(1)} %tmat_apply.3.own_ref.refs_3_), channel_id=1, source_target_pairs={{0,8},{2,10},{4,12},{6,14},{8,0},{10,2},{12,4},{14,6},{16,24},{18,... | collective-permute-start | bytes 393224 | tf_op jit(solution)/shard_map/ppermute | solution.py:451
  11.4 8.3 %collective-permute-start.3 = (f32[2,2,32,256]{3,2,1,0:T(8,128)S(1)}, f32[2,2,32,256]{3,2,1,0:T(8,128)S(1)}, u32[]{:S(2)}, u32[]{:S(2)}) collective-permute-start(f32[2,2,32,256]{3,2,1,0:T(8,128)S(1)} %tmat_apply.3.own_ref.refs_3_), channel_id=1, source_target_pairs={{0,4},{2,6},{4,0},{6,2},{8,12},{10,14},{12,8},{14,10},{16,20},{18,... | collective-permute-start | bytes 393224 | tf_op jit(solution)/shard_map/ppermute | solution.py:451
  12.8 6.9 %collective-permute-start.2 = (f32[2,2,32,256]{3,2,1,0:T(8,128)S(1)}, f32[2,2,32,256]{3,2,1,0:T(8,128)S(1)}, u32[]{:S(2)}, u32[]{:S(2)}) collective-permute-start(f32[2,2,32,256]{3,2,1,0:T(8,128)S(1)} %tmat_apply.3.own_ref.refs_3_), channel_id=1, source_target_pairs={{0,2},{2,0},{4,6},{6,4},{8,10},{10,8},{12,14},{14,12},{16,18},{18,... | collective-permute-start | bytes 393224 | tf_op jit(solution)/shard_map/ppermute | solution.py:451
  19.7 10.9 %collective-permute-start.5 = (f32[5,2,32,256]{3,2,1,0:T(8,128)S(1)}, f32[5,2,32,256]{3,2,1,0:T(8,128)S(1)}, u32[]{:S(2)}, u32[]{:S(2)}) collective-permute-start(f32[5,2,32,256]{3,2,1,0:T(8,128)S(1)} %get-tuple-element.45), channel_id=1, source_target_pairs={{0,2},{2,0},{4,6},{6,4},{8,10},{10,8},{12,14},{14,12},{16,18},{18,... | collective-permute-start | bytes 983048 | tf_op jit(solution)/shard_map/ppermute | solution.py:451
  19.8 10.9 %collective-permute-start.6 = (f32[5,2,32,256]{3,2,1,0:T(8,128)S(1)}, f32[5,2,32,256]{3,2,1,0:T(8,128)S(1)}, u32[]{:S(2)}, u32[]{:S(2)}) collective-permute-start(f32[5,2,32,256]{3,2,1,0:T(8,128)S(1)} %get-tuple-element.46), channel_id=1, source_target_pairs={{0,4},{2,6},{4,0},{6,2},{8,12},{10,14},{12,8},{14,10},{16,20},{18,... | collective-permute-start | bytes 983048 | tf_op jit(solution)/shard_map/ppermute | solution.py:451
  21.6 9.0 %collective-permute-start.7 = (f32[2,2,32,256]{3,2,1,0:T(8,128)S(1)}, f32[2,2,32,256]{3,2,1,0:T(8,128)S(1)}, u32[]{:S(2)}, u32[]{:S(2)}) collective-permute-start(f32[2,2,32,256]{3,2,1,0:T(8,128)S(1)} %get-tuple-element.47), channel_id=1, source_target_pairs={{0,16},{2,18},{4,20},{6,22},{8,24},{10,26},{12,28},{14,30},{16,0},... | collective-permute-start | bytes 393224 | tf_op jit(solution)/shard_map/ppermute | solution.py:451
  30.8 14.1 %collective-permute-start.8 = (f32[8,2,32,256]{3,2,1,0:T(8,128)S(1)}, f32[8,2,32,256]{3,2,1,0:T(8,128)S(1)}, u32[]{:S(2)}, u32[]{:S(2)}) collective-permute-start(f32[8,2,32,256]{3,2,1,0:T(8,128)S(1)} %get-tuple-element.51), channel_id=1, source_target_pairs={{0,2},{2,0},{4,6},{6,4},{8,10},{10,8},{12,14},{14,12},{16,18},{18,... | collective-permute-start | bytes 1572872 | tf_op jit(solution)/shard_map/ppermute | solution.py:451
  30.9 14.5 %collective-permute-start.9 = (f32[8,2,32,256]{3,2,1,0:T(8,128)S(1)}, f32[8,2,32,256]{3,2,1,0:T(8,128)S(1)}, u32[]{:S(2)}, u32[]{:S(2)}) collective-permute-start(f32[8,2,32,256]{3,2,1,0:T(8,128)S(1)} %get-tuple-element.52), channel_id=1, source_target_pairs={{0,4},{2,6},{4,0},{6,2},{8,12},{10,14},{12,8},{14,10},{16,20},{18,... | collective-permute-start | bytes 1572872 | tf_op jit(solution)/shard_map/ppermute | solution.py:451
  35.2 9.7 %collective-permute-start.10 = (f32[2,2,32,256]{3,2,1,0:T(8,128)S(1)}, f32[2,2,32,256]{3,2,1,0:T(8,128)S(1)}, u32[]{:S(2)}, u32[]{:S(2)}) collective-permute-start(f32[2,2,32,256]{3,2,1,0:T(8,128)S(1)} %get-tuple-element.53), channel_id=1, source_target_pairs={{0,16},{2,18},{4,20},{6,22},{8,24},{10,26},{12,28},{14,30},{16,0},... | collective-permute-start | bytes 393224 | tf_op jit(solution)/shard_map/ppermute | solution.py:451
  45.5 8.9 %collective-permute-start.11 = (f32[6,2,32,256]{3,2,1,0:T(8,128)S(1)}, f32[6,2,32,256]{3,2,1,0:T(8,128)S(1)}, u32[]{:S(2)}, u32[]{:S(2)}) collective-permute-start(f32[6,2,32,256]{3,2,1,0:T(8,128)S(1)} %get-tuple-element.55), channel_id=1, source_target_pairs={{0,2},{2,0},{4,6},{6,4},{8,10},{10,8},{12,14},{14,12},{16,18},{18,... | collective-permute-start | bytes 1179656 | tf_op jit(solution)/shard_map/ppermute | solution.py:451
  45.9 8.5 %collective-permute-start.12 = (f32[6,2,32,256]{3,2,1,0:T(8,128)S(1)}, f32[6,2,32,256]{3,2,1,0:T(8,128)S(1)}, u32[]{:S(2)}, u32[]{:S(2)}) collective-permute-start(f32[6,2,32,256]{3,2,1,0:T(8,128)S(1)} %get-tuple-element.56), channel_id=1, source_target_pairs={{0,4},{2,6},{4,0},{6,2},{8,12},{10,14},{12,8},{14,10},{16,20},{18,... | collective-permute-start | bytes 1179656 | tf_op jit(solution)/shard_map/ppermute | solution.py:451
  47.8 14.4 %collective-permute-start.15 = (f32[4,2,32,256]{3,2,1,0:T(8,128)S(1)}, f32[4,2,32,256]{3,2,1,0:T(8,128)S(1)}, u32[]{:S(2)}, u32[]{:S(2)}) collective-permute-start(f32[4,2,32,256]{3,2,1,0:T(8,128)S(1)} %get-tuple-element.61), channel_id=1, source_target_pairs={{0,16},{2,18},{4,20},{6,22},{8,24},{10,26},{12,28},{14,30},{16,0},... | collective-permute-start | bytes 786440 | tf_op jit(solution)/shard_map/ppermute | solution.py:451
  54.4 7.8 %collective-permute-start.13 = (f32[3,2,32,256]{3,2,1,0:T(8,128)S(1)}, f32[3,2,32,256]{3,2,1,0:T(8,128)S(1)}, u32[]{:S(2)}, u32[]{:S(2)}) collective-permute-start(f32[3,2,32,256]{3,2,1,0:T(8,128)S(1)} %get-tuple-element.58), channel_id=1, source_target_pairs={{0,2},{2,0},{4,6},{6,4},{8,10},{10,8},{12,14},{14,12},{16,18},{18,... | collective-permute-start | bytes 589832 | tf_op jit(solution)/shard_map/ppermute | solution.py:451
  56.2 6.1 %collective-permute-start.14 = (f32[3,2,32,256]{3,2,1,0:T(8,128)S(1)}, f32[3,2,32,256]{3,2,1,0:T(8,128)S(1)}, u32[]{:S(2)}, u32[]{:S(2)}) collective-permute-start(f32[3,2,32,256]{3,2,1,0:T(8,128)S(1)} %get-tuple-element.59), channel_id=1, source_target_pairs={{0,4},{2,6},{4,0},{6,2},{8,12},{10,14},{12,8},{14,10},{16,20},{18,... | collective-permute-start | bytes 589832 | tf_op jit(solution)/shard_map/ppermute | solution.py:451
  62.2 5.0 %collective-permute-start.16 = (f32[2,2,32,256]{3,2,1,0:T(8,128)S(1)}, f32[2,2,32,256]{3,2,1,0:T(8,128)S(1)}, u32[]{:S(2)}, u32[]{:S(2)}) collective-permute-start(f32[2,2,32,256]{3,2,1,0:T(8,128)S(1)} %pack_sums.2.refs_4_), channel_id=1, source_target_pairs={{0,8},{2,10},{4,12},{6,14},{8,0},{10,2},{12,4},{14,6},{16,24},{18,... | collective-permute-start | bytes 393224 | tf_op jit(solution)/shard_map/ppermute | solution.py:451
  70.0 5.8 %collective-permute-start.21 = (f32[2,2,32,256]{3,2,1,0:T(8,128)S(1)}, f32[2,2,32,256]{3,2,1,0:T(8,128)S(1)}, u32[]{:S(2)}, u32[]{:S(2)}) collective-permute-start(f32[2,2,32,256]{3,2,1,0:T(8,128)S(1)} %tmat_apply.4.own_ref.refs_3_), channel_id=1, source_target_pairs={{0,8},{2,10},{4,12},{6,14},{8,0},{10,2},{12,4},{14,6},{16,24},{18,... | collective-permute-start | bytes 393224 | tf_op jit(solution)/shard_map/ppermute | solution.py:451
  70.0 5.8 %collective-permute-start.20 = (f32[2,2,32,256]{3,2,1,0:T(8,128)S(1)}, f32[2,2,32,256]{3,2,1,0:T(8,128)S(1)}, u32[]{:S(2)}, u32[]{:S(2)}) collective-permute-start(f32[2,2,32,256]{3,2,1,0:T(8,128)S(1)} %tmat_apply.4.own_ref.refs_3_), channel_id=1, source_target_pairs={{0,4},{2,6},{4,0},{6,2},{8,12},{10,14},{12,8},{14,10},{16,20},{18,... | collective-permute-start | bytes 393224 | tf_op jit(solution)/shard_map/ppermute | solution.py:451
  70.0 5.7 %collective-permute-start.19 = (f32[2,2,32,256]{3,2,1,0:T(8,128)S(1)}, f32[2,2,32,256]{3,2,1,0:T(8,128)S(1)}, u32[]{:S(2)}, u32[]{:S(2)}) collective-permute-start(f32[2,2,32,256]{3,2,1,0:T(8,128)S(1)} %tmat_apply.4.own_ref.refs_3_), channel_id=1, source_target_pairs={{0,2},{2,0},{4,6},{6,4},{8,10},{10,8},{12,14},{14,12},{16,18},{18,... | collective-permute-start | bytes 393224 | tf_op jit(solution)/shard_map/ppermute | solution.py:451
  75.8 10.4 %collective-permute-start.22 = (f32[5,2,32,256]{3,2,1,0:T(8,128)S(1)}, f32[5,2,32,256]{3,2,1,0:T(8,128)S(1)}, u32[]{:S(2)}, u32[]{:S(2)}) collective-permute-start(f32[5,2,32,256]{3,2,1,0:T(8,128)S(1)} %get-tuple-element.62), channel_id=1, source_target_pairs={{0,2},{2,0},{4,6},{6,4},{8,10},{10,8},{12,14},{14,12},{16,18},{18,... | collective-permute-start | bytes 983048 | tf_op jit(solution)/shard_map/ppermute | solution.py:451
  76.6 9.6 %collective-permute-start.23 = (f32[5,2,32,256]{3,2,1,0:T(8,128)S(1)}, f32[5,2,32,256]{3,2,1,0:T(8,128)S(1)}, u32[]{:S(2)}, u32[]{:S(2)}) collective-permute-start(f32[5,2,32,256]{3,2,1,0:T(8,128)S(1)} %get-tuple-element.63), channel_id=1, source_target_pairs={{0,4},{2,6},{4,0},{6,2},{8,12},{10,14},{12,8},{14,10},{16,20},{18,... | collective-permute-start | bytes 983048 | tf_op jit(solution)/shard_map/ppermute | solution.py:451
  77.9 8.3 %collective-permute-start.24 = (f32[2,2,32,256]{3,2,1,0:T(8,128)S(1)}, f32[2,2,32,256]{3,2,1,0:T(8,128)S(1)}, u32[]{:S(2)}, u32[]{:S(2)}) collective-permute-start(f32[2,2,32,256]{3,2,1,0:T(8,128)S(1)} %get-tuple-element.64), channel_id=1, source_target_pairs={{0,16},{2,18},{4,20},{6,22},{8,24},{10,26},{12,28},{14,30},{16,0},... | collective-permute-start | bytes 393224 | tf_op jit(solution)/shard_map/ppermute | solution.py:451
  86.4 13.2 %collective-permute-start.25 = (f32[8,2,32,256]{3,2,1,0:T(8,128)S(1)}, f32[8,2,32,256]{3,2,1,0:T(8,128)S(1)}, u32[]{:S(2)}, u32[]{:S(2)}) collective-permute-start(f32[8,2,32,256]{3,2,1,0:T(8,128)S(1)} %get-tuple-element.66), channel_id=1, source_target_pairs={{0,2},{2,0},{4,6},{6,4},{8,10},{10,8},{12,14},{14,12},{16,18},{18,... | collective-permute-start | bytes 1572872 | tf_op jit(solution)/shard_map/ppermute | solution.py:451
  87.6 12.0 %collective-permute-start.26 = (f32[8,2,32,256]{3,2,1,0:T(8,128)S(1)}, f32[8,2,32,256]{3,2,1,0:T(8,128)S(1)}, u32[]{:S(2)}, u32[]{:S(2)}) collective-permute-start(f32[8,2,32,256]{3,2,1,0:T(8,128)S(1)} %get-tuple-element.67), channel_id=1, source_target_pairs={{0,4},{2,6},{4,0},{6,2},{8,12},{10,14},{12,8},{14,10},{16,20},{18,... | collective-permute-start | bytes 1572872 | tf_op jit(solution)/shard_map/ppermute | solution.py:451
  88.4 9.4 %collective-permute-start.27 = (f32[2,2,32,256]{3,2,1,0:T(8,128)S(1)}, f32[2,2,32,256]{3,2,1,0:T(8,128)S(1)}, u32[]{:S(2)}, u32[]{:S(2)}) collective-permute-start(f32[2,2,32,256]{3,2,1,0:T(8,128)S(1)} %get-tuple-element.68), channel_id=1, source_target_pairs={{0,16},{2,18},{4,20},{6,22},{8,24},{10,26},{12,28},{14,30},{16,0},... | collective-permute-start | bytes 393224 | tf_op jit(solution)/shard_map/ppermute | solution.py:451
  99.7 9.4 %collective-permute-start.28 = (f32[6,2,32,256]{3,2,1,0:T(8,128)S(1)}, f32[6,2,32,256]{3,2,1,0:T(8,128)S(1)}, u32[]{:S(2)}, u32[]{:S(2)}) collective-permute-start(f32[6,2,32,256]{3,2,1,0:T(8,128)S(1)} %get-tuple-element.69), channel_id=1, source_target_pairs={{0,2},{2,0},{4,6},{6,4},{8,10},{10,8},{12,14},{14,12},{16,18},{18,... | collective-permute-start | bytes 1179656 | tf_op jit(solution)/shard_map/ppermute | solution.py:451
  101.5 8.9 %collective-permute-start.29 = (f32[6,2,32,256]{3,2,1,0:T(8,128)S(1)}, f32[6,2,32,256]{3,2,1,0:T(8,128)S(1)}, u32[]{:S(2)}, u32[]{:S(2)}) collective-permute-start(f32[6,2,32,256]{3,2,1,0:T(8,128)S(1)} %get-tuple-element.70), channel_id=1, source_target_pairs={{0,4},{2,6},{4,0},{6,2},{8,12},{10,14},{12,8},{14,10},{16,20},{18,... | collective-permute-start | bytes 1179656 | tf_op jit(solution)/shard_map/ppermute | solution.py:451
  101.7 14.0 %collective-permute-start.32 = (f32[4,2,32,256]{3,2,1,0:T(8,128)S(1)}, f32[4,2,32,256]{3,2,1,0:T(8,128)S(1)}, u32[]{:S(2)}, u32[]{:S(2)}) collective-permute-start(f32[4,2,32,256]{3,2,1,0:T(8,128)S(1)} %get-tuple-element.75), channel_id=1, source_target_pairs={{0,16},{2,18},{4,20},{6,22},{8,24},{10,26},{12,28},{14,30},{16,0},... | collective-permute-start | bytes 786440 | tf_op jit(solution)/shard_map/ppermute | solution.py:451
  110.4 5.7 %collective-permute-start.30 = (f32[3,2,32,256]{3,2,1,0:T(8,128)S(1)}, f32[3,2,32,256]{3,2,1,0:T(8,128)S(1)}, u32[]{:S(2)}, u32[]{:S(2)}) collective-permute-start(f32[3,2,32,256]{3,2,1,0:T(8,128)S(1)} %get-tuple-element.72), channel_id=1, source_target_pairs={{0,2},{2,0},{4,6},{6,4},{8,10},{10,8},{12,14},{14,12},{16,18},{18,... | collective-permute-start | bytes 589832 | tf_op jit(solution)/shard_map/ppermute | solution.py:451
  111.0 5.7 %collective-permute-start.31 = (f32[3,2,32,256]{3,2,1,0:T(8,128)S(1)}, f32[3,2,32,256]{3,2,1,0:T(8,128)S(1)}, u32[]{:S(2)}, u32[]{:S(2)}) collective-permute-start(f32[3,2,32,256]{3,2,1,0:T(8,128)S(1)} %get-tuple-element.73), channel_id=1, source_target_pairs={{0,4},{2,6},{4,0},{6,2},{8,12},{10,14},{12,8},{14,10},{16,20},{18,... | collective-permute-start | bytes 589832 | tf_op jit(solution)/shard_map/ppermute | solution.py:451
  115.8 5.0 %collective-permute-start.33 = (f32[2,2,32,256]{3,2,1,0:T(8,128)S(1)}, f32[2,2,32,256]{3,2,1,0:T(8,128)S(1)}, u32[]{:S(2)}, u32[]{:S(2)}) collective-permute-start(f32[2,2,32,256]{3,2,1,0:T(8,128)S(1)} %pack_sums.3.refs_4_), channel_id=1, source_target_pairs={{0,8},{2,10},{4,12},{6,14},{8,0},{10,2},{12,4},{14,6},{16,24},{18,... | collective-permute-start | bytes 393224 | tf_op jit(solution)/shard_map/ppermute | solution.py:451
  (7 other events, 8.6 us)
